TPU v7x, 32 devices: a whole 2x2x4 slice. The times are simulated.
32 devices in a mesh: groups: 2 (over x), row: 16 (over z, y, core).
Axes of the slice: x: 2, y: 2, z: 4, core: 2. Of those that a mesh axis runs over, the one named last changes fastest.
Arguments:
- samples: bfloat16 [2, 64, 524288], P(None, 'groups', 'row'), parts along dimension 1, may hold values from -6 to 6
- delay_knots: bfloat16 [2, 64, 16], P(None, 'groups', 'row'), parts along dimension 1, may hold values from -3 to 3
- sample_delays: int32 [64, 16], P('groups'), parts along dimension 0, may hold values from 0 to 4095, as said below
- owner_map: int32 [4096], replicated, may hold values from 0 to 4095, each once
- filter_taps: float32 [4, 4096], replicated, may hold values from -3 to 3
Outputs:
- visibilities: float32 [2, 4, 4096, 1024], P(None, 'groups', 'row'), parts along dimension 1
There are 2 independent parts, one for each index of `groups`. A program takes and returns all parts, laid end to end along the dimension named above; an argument that names none is the same for every part. Nothing has to cross between parts.
Inputs may be any that keep to these rules, and one draw needn't show every extreme that they name: `sample_delays`: whole-sample delays; in every draw some entry is 0 and some entry is 4095. `owner_map`: each channel appears exactly once.
All inputs are finite; a program needn't handle non-finite values.
Results may differ from a plain program's by a relative error of at most 0.0025.
Values may be sent and summed in bfloat16 or wider, within the bound.
A program may use at most 192 MiB of HBM per device.

v0:
```python
import math

import jax
import jax.numpy as jnp
from jax import lax
from jax.sharding import PartitionSpec as P

TAPS = 4
DUMP_SEGS = 8


def shifted(block, axis, distance):
    devices = range(lax.axis_size(axis))
    route = [(i - distance, i) for i in devices if i - distance in devices]
    return lax.ppermute(block, axis, route)


def shift_station_rows(window, offsets, length):
    moved_rows = []
    for station in range(window.shape[1]):
        moved_rows.append(
            lax.dynamic_slice_in_dim(window[:, station], offsets[station], length, axis=1)
        )
    return jnp.stack(moved_rows, axis=1)


def block_matrix(size, scale):
    counter = jnp.arange(size, dtype=jnp.int32)
    product = counter[:, None] * counter[None, :] % size
    angle = 2.0 * math.pi / size * product.astype(jnp.float32)
    w_real = jnp.cos(angle) * scale
    w_imag = -jnp.sin(angle) * scale
    return jnp.stack([jnp.stack([w_real, -w_imag]), jnp.stack([w_imag, w_real])])


def shards(samples, delay_knots, sample_delays, owner_map, filter_taps):
    channels = filter_taps.shape[1]
    stations = samples.shape[1]
    seg_len = samples.shape[2]
    frames = seg_len // channels
    history = TAPS - 1
    devices = lax.axis_size("row")
    position = lax.axis_index("row")
    own_delay = lax.dynamic_index_in_dim(sample_delays, position, 1, keepdims=False)
    raw_tail, prev_knots = shifted((samples[:, :, seg_len - channels :], delay_knots), "row", 1)
    window = jnp.concatenate([raw_tail, samples], axis=2)
    delayed = shift_station_rows(window, channels - own_delay, seg_len)
    filter_tail = shifted(delayed[:, :, seg_len - history * channels :], "row", 1)
    extended = jnp.concatenate([filter_tail, delayed], axis=2).reshape(
        2, stations, frames + history, channels
    )
    filtered = sum(
        (
            filter_taps[tap_id] * extended[:, :, tap_id : tap_id + frames].astype(jnp.float32)
            for tap_id in range(TAPS)
        )
    )
    knots_own = delay_knots[:, :, 0].astype(jnp.float32)
    knots_prev = jnp.where(position == 0, knots_own, prev_knots[:, :, 0].astype(jnp.float32))
    weights = (jnp.arange(frames, dtype=jnp.float32) + 1.0) / frames
    track = (1.0 - weights) * knots_prev[..., None] + weights * knots_own[..., None]
    track = track.reshape(2, stations * frames)
    radix_two = 128
    radix_one = channels // radix_two
    section_one = block_matrix(radix_one, 1.0)
    section_two = block_matrix(radix_two, 1.0 / math.sqrt(channels))
    rows_one = jnp.arange(radix_one, dtype=jnp.int32)
    rows_two = jnp.arange(radix_two, dtype=jnp.int32)
    twist = 2.0 * math.pi / channels * (rows_one[:, None] * rows_two[None, :]).astype(jnp.float32)
    twist_table = jnp.stack([jnp.cos(twist), -jnp.sin(twist)])[..., None]
    picked = owner_map % radix_one * radix_two + owner_map // radix_one
    freq = (owner_map.astype(jnp.float32) - channels / 2) / channels
    frame_rows = filtered.reshape(2, stations * frames, radix_one, radix_two)
    first = jnp.einsum("pqca,qnab->pcbn", section_one, frame_rows, precision=lax.Precision.HIGHEST)
    turned_real = first[0] * twist_table[0] - first[1] * twist_table[1]
    turned_imag = first[0] * twist_table[1] + first[1] * twist_table[0]
    turned = jnp.stack([turned_real, turned_imag])
    second = jnp.einsum("pqdb,qcbn->cdpn", section_two, turned, precision=lax.Precision.HIGHEST)
    second = second.reshape(channels, 2, frame_rows.shape[1])
    ordered = jnp.take(second, picked, axis=0)
    angle = (2.0 * math.pi * track[0])[None, :] * freq[:, None] + track[1][None, :]
    cosine = jnp.cos(angle)
    sine = jnp.sin(angle)
    rot_real = ordered[:, 0] * cosine - ordered[:, 1] * sine
    rot_imag = ordered[:, 0] * sine + ordered[:, 1] * cosine
    packed = jnp.stack([rot_real.astype(jnp.bfloat16), rot_imag.astype(jnp.bfloat16)], axis=1)
    packed_all = packed.reshape(devices, channels // devices, 2, frame_rows.shape[1])
    received = lax.all_to_all(packed_all, "row", split_axis=0, concat_axis=0, tiled=True)
    dump_count = received.shape[0] // DUMP_SEGS
    items = received.shape[1]
    arranged = received.reshape(dump_count, DUMP_SEGS, items, 2, stations, frames)
    prods = jnp.einsum(
        "gdcpsf,gdcqtf->pqgcst", arranged, arranged, preferred_element_type=jnp.float32
    )
    vis_real = prods[0, 0] + prods[1, 1]
    vis_imag = prods[1, 0] - prods[0, 1]
    result = jnp.stack([vis_real, vis_imag]) / (DUMP_SEGS * frames)
    return result.reshape(2, dump_count, items, stations * stations)


def solution(mesh):
    placed = (P(None, "groups", "row"), P(None, "groups", "row"), P("groups", None), P(), P())
    return jax.shard_map(
        shards,
        mesh=mesh,
        in_specs=placed,
        out_specs=P(None, "groups", "row", None),
        check_vma=False,
    )
```

profile of v0, /device:TPU:0, one launch (start us, length us, event | category | flops | bytes accessed | tf_op | source)
XLA Modules:
  0.0 524.9 jit_solution(5521798382286132200)
XLA Ops:
  0.0 2.9 collective-permute-start.2
  2.9 1.1 slice.297
  3.9 4.1 collective-permute-start
  8.0 1.2 convert_bitcast_fusion
  9.2 0.7 fusion.40
  9.9 0.7 fusion.47
  26.9 0.7 fusion.46
  51.6 0.3 negate_multiply_fusion
  51.9 0.7 add_multiply_fusion
  72.5 0.6 maximum_bitcast_fusion.7
  73.1 0.7 maximum_bitcast_fusion.3
  73.8 0.7 sine_negate_fusion
  74.5 1.3 compare_and_fusion
  75.8 0.6 broadcast_clamp_fusion
  76.5 2.5 constant_dynamic-update-slice_fusion
  78.9 4.3 fusion.44
  83.2 6.4 %fusion.43 = (bf16[2,1,36864]{2,1,0:T(2,128)(2,1)S(1)}, bf16[2,1,36864]{2,1,0:T(2,128)(2,1)S(1)}, bf16[2,1,36864]{2,1,0:T(2,128)(2,1)S(1)}, bf16[2,1,36864]{2,1,...) fusion(bf16[2,32,36864]{2,1,0:T(8,128)(2,1)S(1)} %constant_dyna, ...), kind=kLoop, calls=%fused_computation.122 | loop fusion | bytes 5603328 | tf_op jit(solution)/shard_map/slice | solution.py:22
  89.7 0.6 constant_dynamic-slice_fusion.19
  90.3 0.6 constant_dynamic-slice_fusion.21
  91.0 0.7 constant_dynamic-slice_fusion.23
  91.7 0.6 constant_dynamic-slice_fusion.25
  92.3 0.6 constant_dynamic-slice_fusion.27
  93.0 0.6 constant_dynamic-slice_fusion.29
  93.6 1.4 constant_dynamic-slice_fusion
  95.0 1.4 constant_dynamic-slice_fusion.18
  96.4 1.4 constant_dynamic-slice_fusion.2
  97.9 1.5 constant_dynamic-slice_fusion.4
  99.3 1.4 constant_dynamic-slice_fusion.6
  100.7 1.4 constant_dynamic-slice_fusion.8
  102.2 1.4 constant_dynamic-slice_fusion.10
  103.6 1.4 constant_dynamic-slice_fusion.12
  105.0 1.4 constant_dynamic-slice_fusion.14
  106.5 1.4 constant_dynamic-slice_fusion.16
  107.9 25.3 %stack.32 = bf16[2,32,32768]{2,1,0:T(8,128)(2,1)} concatenate(bf16[2,1,32768]{2,1,0:T(2,128)(2,1)} %get-tuple-element.120, bf16[2,1,32768]{2,1,0:T(2,128)(2,1)S(1)} %get-tuple-element.100, bf16[2,1,32768]{2,1,0:T(2,128)(2,1)S(1)} %get-tuple-element.99, bf16[2,1,32768]{2,1,0:T(2,128)(2,1)S(1)} %get-tuple-element.98, bf16[2,1,32768]{2,1,0:T(2,128)(2,1)S(1)} %get-tuple-element.97, ...), dimensions={1} | concatenate | bytes 8388608 | tf_op jit(solution)/shard_map/stack | solution.py:24
  133.2 1.5 slice.414
  134.8 1.9 collective-permute-start.1
  136.7 1.1 fusion.45
  137.8 0.7 fusion.39
  138.5 0.7 multiply_add_fusion.3
  139.6 5.1 pad_maximum_fusion
  144.7 9.6 %reshape.552 = bf16[2,32,11,4096]{3,2,1,0:T(8,128)(2,1)} reshape(bf16[2,32,45056]{2,1,0:T(8,128)(2,1)} %pad_maximum_fusion) | data formatting | bytes 11534336 | tf_op jit(solution)/shard_map/reshape | solution.py:49
  154.4 13.3 %multiply_add_fusion = f32[2,32,8,4096]{3,2,1,0:T(8,128)S(1)} fusion(bf16[2,32,11,4096]{3,2,1,0:T(8,128)(2,1)} %reshape.552, f32[4096]{0:T(1024)S(1)} %bitcast.108, f32[4096]{0:T(1024)S(1)} %bitcast.109, f32[4096]{0:T(1024)S(1)} %bitcast.107, f32[4096]{0:T(1024)S(1)} %bitcast.106), kind=kLoop, calls=%fused_computation.11 | loop fusion | flops 23068672 | bytes 25231360 | tf_op jit(solution)/shard_map/add | solution.py:52
  167.7 1.8 copy.65
  169.6 8.5 %fusion.9 = f32[2,32,128,256]{2,1,0,3:T(8,128)S(1)} fusion(f32[1,2,32,32]{3,2,1,0:T(8,128)S(1)} %copy-done.2, f32[1,2,32,32]{3,2,1,0:T(8,128)S(1)} %copy-done.1, f32[2,256,32,128]{3,2,1,0:T(8,128)S(1)} %bitcast.100), kind=kOutput, calls=%fused_computation.23 | convolution fusion | flops 1610616832 | bytes 16793600 | tf_op jit(solution)/shard_map/pqca,qnab->pcbn/dot_general | solution.py:74
  178.1 1.3 multiply_subtract_fusion
  179.5 1.2 maximum_bitcast_fusion
  180.8 13.5 %fusion.6 = f32[32,128,2,256]{3,1,2,0:T(8,128)S(1)} fusion(f32[2,32,128,256,1]{2,1,0,3,4:T(8,128)S(1)} %maximum_bitcast_fusion, f32[1,2,128,128]{3,2,1,0:T(8,128)S(1)} %copy-done, f32[1,2,128,128]{3,2,1,0:T(8,128)S(1)} %get-tuple-element.45), kind=kOutput, calls=%fused_computation.22 | convolution fusion | flops 6442516480 | bytes 17039360 | tf_op jit(solution)/shard_map/pqdb,qcbn->cdpn/dot_general | solution.py:78
  194.3 1.0 copy.40
  195.3 23.6 %copy.41 = f32[4096,2,256]{2,1,0:T(2,128)} copy(f32[4096,2,256]{2,0,1:T(8,128)S(1)} %bitcast.101) | data formatting | bytes 16777216 | tf_op jit(solution)/shard_map/reshape | solution.py:79
  218.8 37.3 %gather_fusion = f32[4096,2,256]{2,1,0:T(2,128)} fusion(f32[4096,2,256]{2,1,0:T(2,128)} %copy.41, s32[4096]{0:T(1024)S(1)} %copy-done.3), kind=kCustom, calls=%fused_computation | custom fusion | bytes 16793600 | tf_op jit(solution)/shard_map/jit(_take)/gather | solution.py:80
  256.2 6.3 %copy_select_fusion = f32[4096,2,256]{2,0,1:T(8,128)S(1)} fusion(f32[4096,2,256]{2,1,0:T(2,128)} %gather_fusion, pred[4096]{0:T(1024)(128)(4,1)S(1)} %copy-done.6), kind=kLoop, calls=%fused_computation.10 | loop fusion | flops 2097152 | bytes 16781312 | tf_op jit(solution)/shard_map/jit(_take)/select_n | solution.py:80
  262.5 17.8 %subtract_convert_fusion = (bf16[4096,1,256]{2,0,1:T(8,128)(2,1)S(1)}, bf16[4096,1,256]{2,0,1:T(8,128)(2,1)S(1)}) fusion(f32[4096,2,256]{2,0,1:T(8,128)S(1)} %copy_select_fusion, f32[256]{0:T(256)S(1)} %add.285, f32[4096]{0:T(1024)S(1)} %add_multiply_fusion, f32[256]{0:T(256)S(1)} %mul.443), kind=kLoop, calls=%fused_computation.16 | loop fusion | flops 10485760 | bytes 12601344 | tf_op jit(solution)/shard_map/convert_element_type | solution.py:86
  280.2 0.4 pad_maximum_fusion.1
  280.6 0.4 copy.43
  281.1 115.1 %all_to_all.5 = bf16[16,256,2,256]{3,1,2,0:T(8,128)(2,1)} all-to-all(bf16[16,256,2,256]{3,1,2,0:T(8,128)(2,1)S(1)} %copy.43), channel_id=1, replica_groups=mesh['groups'=2,'row'=16] {'row'}, dimensions={0} | all-to-all | bytes 8388608 | tf_op jit(solution)/shard_map/all_to_all | solution.py:88
  396.1 6.4 %copy.44 = bf16[16,256,2,256]{1,3,2,0:T(8,128)(2,1)} copy(bf16[16,256,2,256]{3,1,2,0:T(8,128)(2,1)} %all_to_all.5) | data formatting | bytes 8388608 | tf_op jit(solution)/shard_map/all_to_all | solution.py:88
  402.5 28.7 %copy.55 = bf16[2,8,256,2,32,8,1]{4,5,1,3,6,2,0:T(8,128)(2,1)} copy(bf16[2,8,256,2,32,8,1]{2,5,4,3,1,0,6:T(8,128)(2,1)} %bitcast.97) | data formatting | bytes 8388608 | tf_op jit(solution)/shard_map/reshape | solution.py:91
  431.2 28.8 %copy.54 = bf16[2,8,256,2,32,8,1]{4,5,1,6,3,2,0:T(8,128)(2,1)} copy(bf16[2,8,256,2,32,8,1]{2,5,4,3,1,0,6:T(8,128)(2,1)} %bitcast.98) | data formatting | bytes 8388608 | tf_op jit(solution)/shard_map/reshape | solution.py:91
  460.0 21.3 %convolution_bitcast_fusion = f32[2,2,2,256,32,32]{4,5,0,1,3,2:T(8,128)} fusion(bf16[2,8,256,2,32,8,1]{4,5,1,6,3,2,0:T(8,128)(2,1)} %copy.54, bf16[2,8,256,2,32,8,1]{4,5,1,3,6,2,0:T(8,128)(2,1)} %copy.55), kind=kOutput, calls=%fused_computation.1 | convolution fusion | flops 268435456 | bytes 16777216 | tf_op jit(solution)/shard_map/gdcpsf,gdcqtf->pqgcst/dot_general | solution.py:92
  481.3 19.0 %slice_add_fusion = (f32[1,1,2,256,32,32]{4,5,0,1,3,2:T(8,128)}, f32[1,1,2,256,32,32]{4,5,0,1,3,2:T(8,128)}) fusion(f32[2,2,2,256,32,32]{4,5,0,1,3,2:T(8,128)} %convolution_bitcast_fusion), kind=kLoop, calls=%fused_computation.4 | loop fusion | flops 1048576 | bytes 12582912 | tf_op jit(solution)/shard_map/add | solution.py:95
  500.4 7.1 %copy.47 = f32[1,1,2,256,32,32]{3,5,4,2,1,0:T(8,128)S(1)} copy(f32[1,1,2,256,32,32]{4,5,0,1,3,2:T(8,128)} %get-tuple-element.7) | data formatting | bytes 4194304 | tf_op jit(solution)/shard_map/add | solution.py:95
  507.5 7.9 %copy.48 = f32[1,1,2,256,32,32]{3,5,4,2,1,0:T(8,128)} copy(f32[1,1,2,256,32,32]{4,5,0,1,3,2:T(8,128)} %get-tuple-element.8) | data formatting | bytes 4194304 | tf_op jit(solution)/shard_map/sub | solution.py:96
  515.3 3.9 maximum_multiply_fusion
  519.3 5.3 %copy.49 = f32[2,2,256,1024]{3,2,1,0:T(8,128)} copy(f32[2,2,256,1024]{2,3,1,0:T(8,128)} %maximum_multiply_fusion) | data formatting | bytes 8388608 | tf_op jit(solution)/shard_map/div | solution.py:97
  (25 shorter events, 0.9 us)
Async XLA Ops:
  0.0 137.8 %collective-permute-start.2 = (bf16[2,32,1]{1,0,2:T(2,128)(2,1)}, bf16[2,32,1]{1,0,2:T(2,128)(2,1)}, u32[]{:S(2)}, u32[]{:S(2)}) collective-permute-start(bf16[2,32,1]{1,0,2:T(2,128)(2,1)} %param.6), channel_id=1, source_target_pairs={{0,1},{1,2},{2,3},{3,4},{4,5},{5,6},{6,7},{7,8},{8,9},{9,10},{10,1... | collective-permute-start | bytes 392 | tf_op jit(solution)/shard_map/ppermute | solution.py:15
  3.9 72.5 %collective-permute-start = (bf16[2,32,4096]{2,1,0:T(8,128)(2,1)S(1)}, bf16[2,32,4096]{2,1,0:T(8,128)(2,1)S(1)}, u32[]{:S(2)}, u32[]{:S(2)}) collective-permute-start(bf16[2,32,4096]{2,1,0:T(8,128)(2,1)S(1)} %slice.297), channel_id=1, source_target_pairs={{0,1},{1,2},{2,3},{3,4},{4,5},{5,6},{6,7},{7,8},{8,9},{9,10},{10,1... | collective-permute-start | bytes 1572872 | tf_op jit(solution)/shard_map/ppermute | solution.py:15
  134.8 4.9 collective-permute-start.1
  167.7 1.9 copy-start.1
  167.7 1.9 copy-start.2
  169.6 8.5 %copy-start.4 = (f32[32,128]{1,0:T(8,128)S(1)}, f32[32,128]{1,0:T(8,128)}, u32[]{:S(2)}) copy-start(f32[32,128]{1,0:T(8,128)} %get-tuple-element.121) | copy-start | bytes 49156
  169.6 8.5 %copy-start.5 = (f32[32,128]{1,0:T(8,128)S(1)}, f32[32,128]{1,0:T(8,128)}, u32[]{:S(2)}) copy-start(f32[32,128]{1,0:T(8,128)} %get-tuple-element.122) | copy-start | bytes 49156
  179.5 1.3 copy-start
  195.3 23.6 %copy-start.3 = (s32[4096]{0:T(1024)S(1)}, s32[4096]{0:T(1024)}, u32[]{:S(2)}) copy-start(s32[4096]{0:T(1024)} %broadcast_clamp_fusion) | copy-start | bytes 49156
  218.8 37.3 %copy-start.6 = (pred[4096]{0:T(1024)(128)(4,1)S(1)}, pred[4096]{0:T(1024)(128)(4,1)}, u32[]{:S(2)}) copy-start(pred[4096]{0:T(1024)(128)(4,1)} %get-tuple-element.5) | copy-start | bytes 12292
where the time goes:
time: 533 us; the launch traced here: 525 us
  local copies, waits for them, and re-layouts  220 us (41%)
  blocking collectives  115 us (22%)
  other arithmetic  77.1 us (14%)
  between operations  60.3 us (11%)
  matrix products  43.4 us (8%)
  starting transfers between devices  8.88 us (2%)
    all_to_all x1, blocking collectives, shards(): lax.all_to_all(packed_all, 'row', split_axis=0, concat_axis=0, tiled=True)  115 us
    reshape x2, local copies, waits for them, and re-layouts, shards(): received.reshape(dump_count, DUMP_SEGS, items, 2, stations, frames)  57.5 us
    gather x1, local copies, waits for them, and re-layouts, shards(): ordered = jnp.take(second, picked, axis=0)  37.3 us
    another operation x1, local copies, waits for them, and re-layouts, shift_station_rows(): return jnp.stack(moved_rows, axis=1)  25.3 us
    reshape x1, local copies, waits for them, and re-layouts, shards(): second = second.reshape(channels, 2, frame_rows.shape[1])  23.6 us
    dot_general x1, matrix products, shards(): jnp.einsum('gdcpsf,gdcqtf->pqgcst', arranged, arranged, preferred_element...  21.3 us
    add x1, other arithmetic, shards(): vis_real = prods[0, 0] + prods[1, 1]  19 us
    dynamic_slice x16, local copies, waits for them, and re-layouts, shift_station_rows(): lax.dynamic_slice_in_dim(window[:, station], offsets[station], length, ax...  18.2 us
  transfers between devices with their start and end apart: 3, of which 1 were waited for; matrix products, arithmetic and copies ran while one was open for 13% of the time, Pallas kernels for 0%

commit v1 on v0

v1 whole, which is shorter than its diff:
```python
import math

import jax
import jax.numpy as jnp
import numpy as np
from jax import lax
from jax.experimental import pallas as pl
from jax.experimental.pallas import tpu as pltpu
from jax.sharding import PartitionSpec as P

TAPS = 4
DUMP_SEGS = 8
LANES = 128
GROUP = 8


def block_matrix(size, scale):
    counter = np.arange(size)
    angle = 2.0 * math.pi / size * (counter[:, None] * counter[None, :] % size)
    w_real = np.cos(angle) * scale
    w_imag = -np.sin(angle) * scale
    return w_real, w_imag


def split_bf16(values):
    high = values.astype(jnp.bfloat16)
    low = (values - high.astype(jnp.float32)).astype(jnp.bfloat16)
    return high, low


def dot(left, right):
    return jnp.dot(left, right, preferred_element_type=jnp.float32)


def spectra_kernel(
    delays_ref, own_ref, tail_ref, taps_ref, w1h_ref, w1l_ref, twist_ref, w2h_ref, w2l_ref,
    e1_ref, e2_ref, out_ref, window, ext, turned_re, turned_im,
):
    frames = out_ref.shape[1]
    radix = taps_ref.shape[1]
    own_rows = frames * radix
    tail_rows = TAPS * radix
    history = TAPS - 1
    rows = frames * GROUP
    half = frames // 2
    base = pl.program_id(0) * GROUP
    lane = lax.broadcasted_iota(jnp.int32, (1, LANES), 1)

    def shift(part, start, count, where):
        row = start // LANES
        turn = start % LANES
        back = (LANES - turn) % LANES
        near = pltpu.roll(window[part, pl.ds(row, count), :], back, 1)
        far = pltpu.roll(window[part, pl.ds(row + 1, count), :], back, 1)
        ext[part, pl.ds(where, count), :] = jnp.where(lane < LANES - turn, near, far)

    def station(index, carry):
        own_delay = delays_ref[0, base + index]
        prev_delay = delays_ref[1, base + index]
        for part in range(2):
            window[part, 0:tail_rows, :] = tail_ref[part, index].astype(jnp.float32)
            window[part, tail_rows : tail_rows + own_rows, :] = own_ref[part, index].astype(jnp.float32)
            shift(part, radix * LANES - prev_delay, history * radix, 0)
            for frame in range(0, frames, 2):
                shift(
                    part,
                    tail_rows * LANES - own_delay + frame * radix * LANES,
                    2 * radix,
                    (history + frame) * radix,
                )

        def filtered(part, frame):
            total = taps_ref[0] * ext[part, frame * radix : (frame + 1) * radix, :]
            for tap in range(1, TAPS):
                spot = (frame + tap) * radix
                total = total + taps_ref[tap] * ext[part, spot : spot + radix, :]
            return total

        columns = []
        for side in range(2):
            columns.append(
                jnp.concatenate(
                    [filtered(part, side * half + f) for f in range(half) for part in range(2)], axis=0
                )
            )
        high, low = split_bf16(jnp.concatenate(columns, axis=1))
        first = dot(w1h_ref[...], high) + dot(w1h_ref[...], low) + dot(w1l_ref[...], high)
        for side in range(2):
            for f in range(half):
                cols = slice(side * LANES, (side + 1) * LANES)
                real = first[2 * f * radix : (2 * f + 1) * radix, cols]
                imag = first[(2 * f + 1) * radix : (2 * f + 2) * radix, cols]
                place = pl.ds((side * half + f) * GROUP + index, radix, stride=rows)
                turned_re[place, :] = real * twist_ref[0] - imag * twist_ref[1]
                turned_im[place, :] = real * twist_ref[1] + imag * twist_ref[0]
        return carry

    lax.fori_loop(0, GROUP, station, 0)
    batch = 8
    e2_cos = e2_ref[0].reshape(rows, LANES)
    e2_sin = e2_ref[1].reshape(rows, LANES)
    e1_cos = e1_ref[0].reshape(rows, radix)
    e1_sin = e1_ref[1].reshape(rows, radix)
    for start in range(0, radix, batch):
        block = slice(start * rows, (start + batch) * rows)
        high, low = split_bf16(jnp.concatenate([turned_re[block, :], turned_im[block, :]], axis=1))
        second = dot(high, w2h_ref[...]) + dot(low, w2h_ref[...]) + dot(high, w2l_ref[...])
        for step in range(batch):
            c1 = start + step
            real = second[step * rows : (step + 1) * rows, :LANES]
            imag = second[step * rows : (step + 1) * rows, LANES:]
            one_cos = e1_cos[:, c1 : c1 + 1]
            one_sin = e1_sin[:, c1 : c1 + 1]
            cosine = e2_cos * one_cos - e2_sin * one_sin
            sine = e2_sin * one_cos + e2_cos * one_sin
            cols = slice(c1 * LANES, (c1 + 1) * LANES)
            shape = (frames, GROUP, LANES)
            out_ref[0, :, :, cols] = (real * cosine - imag * sine).reshape(shape).astype(jnp.bfloat16)
            out_ref[1, :, :, cols] = (real * sine + imag * cosine).reshape(shape).astype(jnp.bfloat16)


def reorder_kernel(picked_ref, rot_ref, out_ref):
    channels = rot_ref.shape[1]
    tile = out_ref.shape[2]
    chunk = 512
    total = None
    for start in range(0, channels, chunk):
        counter = lax.broadcasted_iota(jnp.int32, (chunk, tile), 0) + start
        hot = jnp.where(counter == picked_ref[0], 1.0, 0.0).astype(jnp.bfloat16)
        term = dot(rot_ref[:, start : start + chunk], hot)
        total = term if total is None else total + term
    out_ref[0] = total.astype(jnp.bfloat16)


def correlate_kernel(data_ref, out_ref, data, acc):
    segs, parts, frames, stations, tile = data_ref.shape
    count = segs * frames
    for part in range(2):
        data[part] = data_ref[:, part].reshape(count, stations, tile).astype(jnp.float32)
    scale = 1.0 / count
    sub = 8

    for tile_a in range(stations // sub):
        low = tile_a * sub
        width = stations - low

        def one_row(pair, carry):
            mine = [low + 2 * pair, low + 2 * pair + 1]

            def frame_step(f, sums):
                b_re = data[0, f, low:, :]
                b_im = data[1, f, low:, :]
                result = []
                for slot, a in enumerate(mine):
                    a_re = data[0, f, pl.ds(a, 1), :]
                    a_im = data[1, f, pl.ds(a, 1), :]
                    result.append(sums[2 * slot] + (a_re * b_re + a_im * b_im))
                    result.append(sums[2 * slot + 1] + (a_im * b_re - a_re * b_im))
                return tuple(result)

            zero = jnp.zeros((width, tile), jnp.float32)
            sums = lax.fori_loop(0, count, frame_step, (zero,) * 4, unroll=4)
            for slot, a in enumerate(mine):
                place = pl.ds(pl.multiple_of(a * stations + low, 8), width)
                acc[0, place, :] = sums[2 * slot] * scale
                acc[1, place, :] = sums[2 * slot + 1] * scale
            return carry

        lax.fori_loop(0, sub // 2, one_row, 0)
    for a in range(sub, stations):
        for low in range(0, a // sub * sub, sub):
            mirror = pl.ds(low * stations + a, sub, stride=stations)
            spot = a * stations + low
            acc[0, spot : spot + sub, :] = acc[0, mirror, :]
            acc[1, spot : spot + sub, :] = -acc[1, mirror, :]
    for part in range(2):
        for start in range(0, stations * stations, LANES):
            out_ref[part, 0, :, start : start + LANES] = acc[part, start : start + LANES, :].T


def shards(samples, delay_knots, sample_delays, owner_map, filter_taps):
    channels = filter_taps.shape[1]
    stations = samples.shape[1]
    seg_len = samples.shape[2]
    frames = seg_len // channels
    devices = lax.axis_size("row")
    position = lax.axis_index("row")
    radix = channels // LANES
    items = channels // devices
    tail_len = TAPS * channels
    route = [(i, i + 1) for i in range(devices - 1)]
    tail, prev_knots = lax.ppermute((samples[:, :, seg_len - tail_len :], delay_knots), "row", route)
    delays = jnp.stack(
        [
            lax.dynamic_index_in_dim(sample_delays, position, 1, keepdims=False),
            lax.dynamic_index_in_dim(sample_delays, jnp.maximum(position - 1, 0), 1, keepdims=False),
        ]
    )
    knots_own = delay_knots[:, :, 0].astype(jnp.float32)
    knots_prev = jnp.where(position == 0, knots_own, prev_knots[:, :, 0].astype(jnp.float32))
    weights = ((jnp.arange(frames, dtype=jnp.float32) + 1.0) / frames)[:, None]
    track = (1.0 - weights) * knots_prev[:, None] + weights * knots_own[:, None]
    turn = 2.0 * math.pi * track[0][..., None]
    coarse = (jnp.arange(LANES, dtype=jnp.float32) * radix - channels / 2) / channels
    fine = jnp.arange(radix, dtype=jnp.float32) / channels
    angle_two = turn * coarse + track[1][..., None]
    angle_one = turn * fine
    e2 = jnp.stack([jnp.cos(angle_two), jnp.sin(angle_two)])
    e1 = jnp.stack([jnp.cos(angle_one), jnp.sin(angle_one)])

    w_real, w_imag = block_matrix(radix, 1.0)
    section_one = np.block([[w_real, -w_imag], [w_imag, w_real]])
    section_one = np.kron(np.eye(frames // 2), section_one).astype(np.float32)
    w_real, w_imag = block_matrix(LANES, 1.0 / math.sqrt(channels))
    section_two = np.block([[w_real, w_imag], [-w_imag, w_real]]).astype(np.float32)
    w1h = section_one.astype(jnp.bfloat16)
    w1l = (section_one - w1h.astype(np.float32)).astype(jnp.bfloat16)
    w2h = section_two.astype(jnp.bfloat16)
    w2l = (section_two - w2h.astype(np.float32)).astype(jnp.bfloat16)
    twist = 2.0 * math.pi / channels * (np.arange(radix)[:, None] * np.arange(LANES)[None, :])
    twist = np.stack([np.cos(twist), -np.sin(twist)]).astype(np.float32)

    rows = frames * GROUP
    whole = lambda *shape: pl.BlockSpec(shape, lambda g: (0,) * len(shape))
    rotated = pl.pallas_call(
        spectra_kernel,
        grid=(stations // GROUP,),
        in_specs=[
            pl.BlockSpec(memory_space=pltpu.SMEM),
            pl.BlockSpec((2, GROUP, frames * radix, LANES), lambda g: (0, g, 0, 0)),
            pl.BlockSpec((2, GROUP, TAPS * radix, LANES), lambda g: (0, g, 0, 0)),
            whole(TAPS, radix, LANES),
            whole(*w1h.shape),
            whole(*w1l.shape),
            whole(2, radix, LANES),
            whole(*w2h.shape),
            whole(*w2l.shape),
            pl.BlockSpec((2, frames, GROUP, radix), lambda g: (0, 0, g, 0)),
            pl.BlockSpec((2, frames, GROUP, LANES), lambda g: (0, 0, g, 0)),
        ],
        out_specs=pl.BlockSpec((2, frames, GROUP, channels), lambda g: (0, 0, g, 0)),
        out_shape=jax.ShapeDtypeStruct((2, frames, stations, channels), jnp.bfloat16),
        scratch_shapes=[
            pltpu.VMEM((2, (frames + TAPS) * radix + 8, LANES), jnp.float32),
            pltpu.VMEM((2, (frames + TAPS - 1) * radix, LANES), jnp.float32),
            pltpu.VMEM((radix * rows, LANES), jnp.float32),
            pltpu.VMEM((radix * rows, LANES), jnp.float32),
        ],
        compiler_params=pltpu.CompilerParams(vmem_limit_bytes=40 * 2**20),
    )(
        delays,
        samples.reshape(2, stations, frames * radix, LANES),
        tail.reshape(2, stations, TAPS * radix, LANES),
        filter_taps.reshape(TAPS, radix, LANES),
        w1h, w1l, twist, w2h, w2l, e1, e2,
    )

    lines = 2 * frames * stations
    picked = (owner_map % radix * LANES + owner_map // radix).reshape(devices, 1, items)
    packed = pl.pallas_call(
        reorder_kernel,
        grid=(devices,),
        in_specs=[
            pl.BlockSpec((1, 1, items), lambda d: (d, 0, 0)),
            pl.BlockSpec((lines, channels), lambda d: (0, 0)),
        ],
        out_specs=pl.BlockSpec((1, lines, items), lambda d: (d, 0, 0)),
        out_shape=jax.ShapeDtypeStruct((devices, lines, items), jnp.bfloat16),
        compiler_params=pltpu.CompilerParams(vmem_limit_bytes=40 * 2**20),
    )(picked, rotated.reshape(lines, channels))

    received = lax.all_to_all(packed, "row", split_axis=0, concat_axis=0, tiled=True)
    received = received.reshape(devices, 2, frames, stations, items)
    dump_count = devices // DUMP_SEGS
    tile = min(LANES, items)
    return pl.pallas_call(
        correlate_kernel,
        grid=(dump_count, items // tile),
        in_specs=[
            pl.BlockSpec((DUMP_SEGS, 2, frames, stations, tile), lambda g, m: (g, 0, 0, 0, m)),
        ],
        out_specs=pl.BlockSpec((2, 1, tile, stations * stations), lambda g, m: (0, g, m, 0)),
        out_shape=jax.ShapeDtypeStruct((2, dump_count, items, stations * stations), jnp.float32),
        scratch_shapes=[
            pltpu.VMEM((2, DUMP_SEGS * frames, stations, tile), jnp.float32),
            pltpu.VMEM((2, stations * stations, tile), jnp.float32),
        ],
        compiler_params=pltpu.CompilerParams(vmem_limit_bytes=40 * 2**20),
    )(received)


def solution(mesh):
    placed = (P(None, "groups", "row"), P(None, "groups", "row"), P("groups", None), P(), P())
    return jax.shard_map(
        shards,
        mesh=mesh,
        in_specs=placed,
        out_specs=P(None, "groups", "row", None),
        check_vma=False,
    )
```

time: 533 us -> 216 us (0.41); the launches traced: 525 us -> 216 us
  local copies, waits for them, and re-layouts: 220 us -> 9.95 us
  Pallas kernels: 0 us -> 83 us
  other arithmetic: 77.1 us -> 1.29 us
  between operations: 60.3 us -> 0.25 us
  matrix products: 43.4 us -> 0 us
    reshape x4 -> x0, local copies, waits for them, and re-layouts: 90.6 us -> none  [the longest x2 57.5 us: shards(): received.reshape(dump_count, DUMP_SEGS, items, 2, stations, frames)]
    pallas_call x0 -> x3, Pallas kernels: none -> 83 us  [the longest x1 31.8 us: shards(): pl.pallas_call(correlate_kernel, grid=(dump_count, items // tile), in_spe...]
    dot_general x3 -> x0, matrix products: 43.4 us -> none  [the longest x1 21.3 us: shards(): jnp.einsum('gdcpsf,gdcqtf->pqgcst', arranged, arranged, preferred_element...]
    gather x1 -> x0, local copies, waits for them, and re-layouts: 37.3 us -> none  [shards(): ordered = jnp.take(second, picked, axis=0)]
    add x3, other arithmetic: 33.1 us -> 0.1 us  [the longest x1 0.07 us: shards(): track = (1.0 - weights) * knots_prev[:, None] + weights * knots_own[:, None]]
    another operation x2 -> x1, local copies, waits for them, and re-layouts: 25.8 us -> 0.87 us  [shards(): jnp.stack([lax.dynamic_index_in_dim(sample_delays, position, 1, keepdims=...]
    dynamic_slice x16 -> x0, local copies, waits for them, and re-layouts: 18.2 us -> none  [shift_station_rows(): lax.dynamic_slice_in_dim(window[:, station], offsets[station], length, ax...]
    convert_element_type x1, other arithmetic: 17.8 us -> 0.01 us  [shards(): knots_own = delay_knots[:, :, 0].astype(jnp.float32)]
  transfers between devices with their start and end apart: 3 -> 2, of which waited for: 1 -> 0; matrix products, arithmetic and copies ran while one was open for 13% -> 5% of each run, Pallas kernels for 0% -> 0%
where the time goes in v1:
time: 216 us
  blocking collectives  114 us (53%)
  Pallas kernels  83 us (38%)
  local copies, waits for them, and re-layouts  9.95 us (5%)
  starting transfers between devices  7.01 us (3%)
    all_to_all x1, blocking collectives, shards(): lax.all_to_all(packed, 'row', split_axis=0, concat_axis=0, tiled=True)  114 us
    pallas_call x1, Pallas kernels, shards(): pl.pallas_call(correlate_kernel, grid=(dump_count, items // tile), in_spe...  31.8 us
    pallas_call x1, Pallas kernels, shards(): pl.pallas_call(spectra_kernel, grid=(stations // GROUP,), in_specs=[pl.Bl...  30.9 us
    pallas_call x1, Pallas kernels, shards(): pl.pallas_call(reorder_kernel, grid=(devices,), in_specs=[pl.BlockSpec((1...  20.2 us
    ppermute x2, starting transfers between devices, shards(): lax.ppermute((samples[:, :, seg_len - tail_len:], delay_knots), 'row', ro...  7.01 us
    unnamed x21, local copies, waits for them, and re-layouts  6.02 us
  transfers between devices with their start and end apart: 2, of which 0 were waited for; matrix products, arithmetic and copies ran while one was open for 5% of the time, Pallas kernels for 0%

profile of v1, /device:TPU:0, one launch (start us, length us, event | category | flops | bytes accessed | tf_op | source)
XLA Modules:
  0.0 215.8 jit_solution(7613960804723457687)
XLA Ops:
  0.0 2.3 %collective-permute-start.1 = (bf16[2,32,1]{1,0,2:T(2,128)(2,1)}, bf16[2,32,1]{1,0,2:T(2,128)(2,1)S(1)}, u32[]{:S(2)}, u32[]{:S(2)}) collective-permute-start(bf16[2,32,1]{1,0,2:T(2,128)(2,1)} %param.11), channel_id=1, source_target_pairs={{0,1},{1,2},{2,3},{3,4},{4,5},{5,6},{6,7},{7,8},{8,9},{9,10},{10,1... | collective-permute-start | bytes 392 | tf_op jit(solution)/shard_map/ppermute | solution.py:192
  2.4 3.1 %slice.9 = bf16[2,32,16384]{2,1,0:T(8,128)(2,1)} slice(bf16[2,32,32768]{2,1,0:T(8,128)(2,1)} %param.10), slice={[0:2], [0:32], [16384:32768]} | slice | bytes 4194304 | tf_op jit(solution)/shard_map/slice | solution.py:192
  5.4 4.7 %collective-permute-start = (bf16[2,32,16384]{2,1,0:T(8,128)(2,1)}, bf16[2,32,16384]{2,1,0:T(8,128)(2,1)S(1)}, u32[]{:S(2)}, u32[]{:S(2)}) collective-permute-start(bf16[2,32,16384]{2,1,0:T(8,128)(2,1)} %slice.9), channel_id=1, source_target_pairs={{0,1},{1,2},{2,3},{3,4},{4,5},{5,6},{6,7},{7,8},{8,9},{9,10},{10,1... | collective-permute-start | bytes 6291464 | tf_op jit(solution)/shard_map/ppermute | solution.py:192
  10.1 0.0 copy-start.8
  10.1 0.0 copy-start.7
  10.2 0.0 copy-start.6
  10.2 5.4 %copy.11 = bf16[8,8,256,128]{3,2,1,0:T(8,128)(2,1)} copy(bf16[8,8,256,128]{3,1,2,0:T(8,128)(2,1)} %bitcast.37) | data formatting | bytes 8388608
  15.6 0.0 copy-start.1
  15.6 0.0 copy-start.2
  15.6 0.0 copy-start.3
  15.6 0.0 copy-start.4
  15.6 0.0 copy-start.5
  15.6 0.0 copy-start
  15.6 0.9 dynamic-slice_bitcast_fusion.1
  16.5 0.0 copy-done.8
  16.5 0.0 copy-done.7
  16.5 0.0 copy-done.6
  16.6 0.0 collective-permute-done.1
  16.6 0.1 multiply_add_fusion.1
  16.7 0.6 fusion.1
  17.3 0.5 multiply_cosine_fusion
  17.8 0.0 collective-permute-done
  17.9 0.6 copy.12
  18.4 0.0 copy-done.1
  18.4 0.0 copy-done.2
  18.4 0.0 copy-done.3
  18.5 0.0 copy-done.4
  18.5 0.0 copy-done.5
  18.5 0.0 copy-done
  18.5 30.9 %shard_map.100 = bf16[2,8,32,4096]{3,2,1,0:T(8,128)(2,1)S(1)} custom-call(s32[2,32]{1,0:T(2,128)S(1)} %pad_add_fusion.delays_ref, bf16[2,32,256,128]{3,2,1,0:T(8,128)(2,1)S(1)} %bitcast.31, bf16[2,32,128,128]{3,2,1,0:T(8,128)(2,1)S(1)} %bitcast.34, f32[4,32,128]{2,1,0:T(8,128)S(1)} %bitcast.35, bf16[256,256]{1,0:T(8,128)(2,1)S(1)} %copy-done.1, ...), custom_call_target="tpu_custom_call" | custom-call | tf_op jit(solution)/shard_map/pallas_call | solution.py:225
  49.4 20.2 %shard_map.101 = bf16[16,512,256]{2,1,0:T(8,128)(2,1)S(1)} custom-call(s32[16,1,256]{2,1,0:T(1,128)S(1)} %bitcast.36, bf16[512,4096]{1,0:T(8,128)(2,1)S(1)} %bitcast.32), custom_call_target="tpu_custom_call" | custom-call | tf_op jit(solution)/shard_map/pallas_call | solution.py:260
  69.7 114.3 %all_to_all.5 = bf16[16,512,256]{2,1,0:T(8,128)(2,1)S(1)} all-to-all(bf16[16,512,256]{2,1,0:T(8,128)(2,1)S(1)} %shard_map.101), channel_id=1, replica_groups=mesh['groups'=2,'row'=16] {'row'}, dimensions={0} | all-to-all | bytes 8388608 | tf_op jit(solution)/shard_map/all_to_all | solution.py:272
  184.0 31.8 %shard_map.102 = f32[2,2,256,1024]{3,2,1,0:T(8,128)} custom-call(bf16[16,2,8,32,256]{4,3,2,1,0:T(8,128)(2,1)S(1)} %bitcast.33), custom_call_target="tpu_custom_call" | custom-call | tf_op jit(solution)/shard_map/pallas_call | solution.py:276
  (11 shorter events, 0.1 us)
Async XLA Ops:
  0.0 16.6 %collective-permute-start.1 = (bf16[2,32,1]{1,0,2:T(2,128)(2,1)}, bf16[2,32,1]{1,0,2:T(2,128)(2,1)S(1)}, u32[]{:S(2)}, u32[]{:S(2)}) collective-permute-start(bf16[2,32,1]{1,0,2:T(2,128)(2,1)} %param.11), channel_id=1, source_target_pairs={{0,1},{1,2},{2,3},{3,4},{4,5},{5,6},{6,7},{7,8},{8,9},{9,10},{10,1... | collective-permute-start | bytes 392 | tf_op jit(solution)/shard_map/ppermute | solution.py:192
  5.4 12.4 %collective-permute-start = (bf16[2,32,16384]{2,1,0:T(8,128)(2,1)}, bf16[2,32,16384]{2,1,0:T(8,128)(2,1)S(1)}, u32[]{:S(2)}, u32[]{:S(2)}) collective-permute-start(bf16[2,32,16384]{2,1,0:T(8,128)(2,1)} %slice.9), channel_id=1, source_target_pairs={{0,1},{1,2},{2,3},{3,4},{4,5},{5,6},{6,7},{7,8},{8,9},{9,10},{10,1... | collective-permute-start | bytes 6291464 | tf_op jit(solution)/shard_map/ppermute | solution.py:192
  10.1 6.4 %copy-start.8 = (bf16[2,32,1]{1,0,2:T(2,128)(2,1)S(1)}, bf16[2,32,1]{1,0,2:T(2,128)(2,1)}, u32[]{:S(2)}) copy-start(bf16[2,32,1]{1,0,2:T(2,128)(2,1)} %param.11) | copy-start | bytes 388
  10.1 6.4 %copy-start.7 = (s32[4096]{0:T(1024)S(1)}, s32[4096]{0:T(1024)}, u32[]{:S(2)}) copy-start(s32[4096]{0:T(1024)} %param.13) | copy-start | bytes 49156
  10.2 6.4 %copy-start.6 = (f32[4,4096]{1,0:T(4,128)S(1)}, f32[4,4096]{1,0:T(4,128)}, u32[]{:S(2)}) copy-start(f32[4,4096]{1,0:T(4,128)} %param.14) | copy-start | bytes 196612
  15.6 2.9 %copy-start.1 = (bf16[256,256]{1,0:T(8,128)(2,1)S(1)}, bf16[256,256]{1,0:T(8,128)(2,1)}, u32[]{:S(2)}) copy-start(bf16[256,256]{1,0:T(8,128)(2,1)} %constant.73.clone.w1h_ref) | copy-start | bytes 393220
  15.6 2.9 %copy-start.2 = (bf16[256,256]{1,0:T(8,128)(2,1)S(1)}, bf16[256,256]{1,0:T(8,128)(2,1)}, u32[]{:S(2)}) copy-start(bf16[256,256]{1,0:T(8,128)(2,1)} %constant.74.clone.w1l_ref) | copy-start | bytes 393220
  15.6 2.9 %copy-start.3 = (bf16[256,256]{1,0:T(8,128)(2,1)S(1)}, bf16[256,256]{1,0:T(8,128)(2,1)}, u32[]{:S(2)}) copy-start(bf16[256,256]{1,0:T(8,128)(2,1)} %constant.76.clone.w2h_ref) | copy-start | bytes 393220
  15.6 2.9 %copy-start.4 = (bf16[256,256]{1,0:T(8,128)(2,1)S(1)}, bf16[256,256]{1,0:T(8,128)(2,1)}, u32[]{:S(2)}) copy-start(bf16[256,256]{1,0:T(8,128)(2,1)} %constant.77.clone.w2l_ref) | copy-start | bytes 393220
  15.6 2.9 %copy-start.5 = (f32[2,32,128]{2,1,0:T(8,128)S(1)}, f32[2,32,128]{2,1,0:T(8,128)}, u32[]{:S(2)}) copy-start(f32[2,32,128]{2,1,0:T(8,128)} %constant.75.clone.twist_ref) | copy-start | bytes 98308
  15.6 2.9 %copy-start = (bf16[8,8,256,128]{3,2,1,0:T(8,128)(2,1)S(1)}, bf16[8,8,256,128]{3,2,1,0:T(8,128)(2,1)}, u32[]{:S(2)}) copy-start(bf16[8,8,256,128]{3,2,1,0:T(8,128)(2,1)} %copy.11) | copy-start | bytes 12582916

commit v2 on v1

--- a/solution.py
+++ b/solution.py
@@ -1,4 +1,5 @@
 import math
+from functools import partial
 
 import jax
 import jax.numpy as jnp
@@ -12,6 +13,7 @@
 DUMP_SEGS = 8
 LANES = 128
 GROUP = 8
+SUB = 8
 
 
 def block_matrix(size, scale):
@@ -33,7 +35,7 @@
 
 
 def spectra_kernel(
-    delays_ref, own_ref, tail_ref, taps_ref, w1h_ref, w1l_ref, twist_ref, w2h_ref, w2l_ref,
+    which, delays_ref, own_ref, tail_ref, taps_ref, w1h_ref, w1l_ref, twist_ref, w2h_ref, w2l_ref,
     e1_ref, e2_ref, out_ref, window, ext, turned_re, turned_im,
 ):
     frames = out_ref.shape[1]
@@ -56,7 +58,7 @@
 
     def station(index, carry):
         own_delay = delays_ref[0, base + index]
-        prev_delay = delays_ref[1, base + index]
+        prev_delay = delays_ref[which, base + index]
         for part in range(2):
             window[part, 0:tail_rows, :] = tail_ref[part, index].astype(jnp.float32)
             window[part, tail_rows : tail_rows + own_rows, :] = own_ref[part, index].astype(jnp.float32)
@@ -119,29 +121,33 @@
             out_ref[1, :, :, cols] = (real * sine + imag * cosine).reshape(shape).astype(jnp.bfloat16)
 
 
-def reorder_kernel(picked_ref, rot_ref, out_ref):
-    channels = rot_ref.shape[1]
+def reorder_kernel(picked_ref, early_ref, late_ref, out_ref):
+    lines, channels = early_ref.shape
     tile = out_ref.shape[2]
     chunk = 512
-    total = None
+    totals = [None, None]
     for start in range(0, channels, chunk):
         counter = lax.broadcasted_iota(jnp.int32, (chunk, tile), 0) + start
         hot = jnp.where(counter == picked_ref[0], 1.0, 0.0).astype(jnp.bfloat16)
-        term = dot(rot_ref[:, start : start + chunk], hot)
-        total = term if total is None else total + term
-    out_ref[0] = total.astype(jnp.bfloat16)
+        for side, ref in enumerate((early_ref, late_ref)):
+            term = dot(ref[:, start : start + chunk], hot)
+            totals[side] = term if totals[side] is None else totals[side] + term
+    out_ref[0, :lines] = totals[0].astype(jnp.bfloat16)
+    out_ref[0, lines:] = totals[1].astype(jnp.bfloat16)
 
 
 def correlate_kernel(data_ref, out_ref, data, acc):
-    segs, parts, frames, stations, tile = data_ref.shape
-    count = segs * frames
+    segs, halves, parts, frames, stations, tile = data_ref.shape
+    count = segs * halves * frames
+    part_count = segs * frames
     for part in range(2):
-        data[part] = data_ref[:, part].reshape(count, stations, tile).astype(jnp.float32)
+        for side in range(halves):
+            block = data_ref[:, side, part].reshape(part_count, stations, tile)
+            data[part, side * part_count : (side + 1) * part_count] = block.astype(jnp.float32)
     scale = 1.0 / count
-    sub = 8
-
-    for tile_a in range(stations // sub):
-        low = tile_a * sub
+
+    for tile_a in range(stations // SUB):
+        low = tile_a * SUB
         width = stations - low
 
         def one_row(pair, carry):
@@ -166,15 +172,45 @@
                 acc[1, place, :] = sums[2 * slot + 1] * scale
             return carry
 
-        lax.fori_loop(0, sub // 2, one_row, 0)
-    for a in range(sub, stations):
-        for low in range(0, a // sub * sub, sub):
-            mirror = pl.ds(low * stations + a, sub, stride=stations)
+        lax.fori_loop(0, SUB // 2, one_row, 0)
+    diagonal = acc[0, pl.ds(0, stations, stride=stations + 1), :]
+    line = lax.broadcasted_iota(jnp.int32, (SUB, tile), 0)
+    for a in range(stations):
+        own = a // SUB * SUB
+        for low in range(0, own, SUB):
             spot = a * stations + low
-            acc[0, spot : spot + sub, :] = acc[0, mirror, :]
-            acc[1, spot : spot + sub, :] = -acc[1, mirror, :]
+            acc[0, spot : spot + SUB, :] = -acc[1, pl.ds(low * stations + a, SUB, stride=stations), :]
+        spot = slice(a * stations + own, a * stations + own + SUB)
+        acc[0, spot, :] = jnp.where(line + own >= a, acc[0, spot, :], acc[1, spot, :])
+    pairs = stations * stations
+    out_ref[0, :pairs, :] = acc[0].astype(jnp.bfloat16)
+    out_ref[0, pairs:, :] = split_bf16(diagonal)[1]
+
+
+def spread_kernel(packed_ref, out_ref, packed, acc):
+    tile = packed_ref.shape[2]
+    pairs = acc.shape[1]
+    stations = packed_ref.shape[1] - pairs
+    packed[...] = packed_ref[0].astype(jnp.float32)
+    line = lax.broadcasted_iota(jnp.int32, (SUB, tile), 0)
+    for a in range(stations):
+        for low in range(0, stations, SUB):
+            spot = slice(a * stations + low, a * stations + low + SUB)
+            direct = packed[spot, :]
+            mirror = packed[pl.ds(low * stations + a, SUB, stride=stations), :]
+            if low > a:
+                real, imag = direct, -mirror
+            elif low + SUB <= a:
+                real, imag = mirror, direct
+            else:
+                fix = packed[pairs + a : pairs + a + 1, :]
+                b = line + low
+                real = jnp.where(b >= a, direct, mirror) + jnp.where(b == a, fix, 0.0)
+                imag = jnp.where(b < a, direct, jnp.where(b == a, 0.0, -mirror))
+            acc[0, spot, :] = real
+            acc[1, spot, :] = imag
     for part in range(2):
-        for start in range(0, stations * stations, LANES):
+        for start in range(0, pairs, LANES):
             out_ref[part, 0, :, start : start + LANES] = acc[part, start : start + LANES, :].T
 
 
@@ -210,7 +246,7 @@
 
     w_real, w_imag = block_matrix(radix, 1.0)
     section_one = np.block([[w_real, -w_imag], [w_imag, w_real]])
-    section_one = np.kron(np.eye(frames // 2), section_one).astype(np.float32)
+    section_one = np.kron(np.eye(frames // 4), section_one).astype(np.float32)
     w_real, w_imag = block_matrix(LANES, 1.0 / math.sqrt(channels))
     section_two = np.block([[w_real, w_imag], [-w_imag, w_real]]).astype(np.float32)
     w1h = section_one.astype(jnp.bfloat16)
@@ -220,73 +256,111 @@
     twist = 2.0 * math.pi / channels * (np.arange(radix)[:, None] * np.arange(LANES)[None, :])
     twist = np.stack([np.cos(twist), -np.sin(twist)]).astype(np.float32)
 
-    rows = frames * GROUP
+    part_frames = frames // 2
+    rows = part_frames * GROUP
+    part_rows = part_frames * radix
     whole = lambda *shape: pl.BlockSpec(shape, lambda g: (0,) * len(shape))
-    rotated = pl.pallas_call(
-        spectra_kernel,
-        grid=(stations // GROUP,),
-        in_specs=[
-            pl.BlockSpec(memory_space=pltpu.SMEM),
-            pl.BlockSpec((2, GROUP, frames * radix, LANES), lambda g: (0, g, 0, 0)),
-            pl.BlockSpec((2, GROUP, TAPS * radix, LANES), lambda g: (0, g, 0, 0)),
-            whole(TAPS, radix, LANES),
-            whole(*w1h.shape),
-            whole(*w1l.shape),
-            whole(2, radix, LANES),
-            whole(*w2h.shape),
-            whole(*w2l.shape),
-            pl.BlockSpec((2, frames, GROUP, radix), lambda g: (0, 0, g, 0)),
-            pl.BlockSpec((2, frames, GROUP, LANES), lambda g: (0, 0, g, 0)),
-        ],
-        out_specs=pl.BlockSpec((2, frames, GROUP, channels), lambda g: (0, 0, g, 0)),
-        out_shape=jax.ShapeDtypeStruct((2, frames, stations, channels), jnp.bfloat16),
-        scratch_shapes=[
-            pltpu.VMEM((2, (frames + TAPS) * radix + 8, LANES), jnp.float32),
-            pltpu.VMEM((2, (frames + TAPS - 1) * radix, LANES), jnp.float32),
-            pltpu.VMEM((radix * rows, LANES), jnp.float32),
-            pltpu.VMEM((radix * rows, LANES), jnp.float32),
-        ],
-        compiler_params=pltpu.CompilerParams(vmem_limit_bytes=40 * 2**20),
-    )(
-        delays,
-        samples.reshape(2, stations, frames * radix, LANES),
-        tail.reshape(2, stations, TAPS * radix, LANES),
-        filter_taps.reshape(TAPS, radix, LANES),
-        w1h, w1l, twist, w2h, w2l, e1, e2,
-    )
-
-    lines = 2 * frames * stations
-    picked = (owner_map % radix * LANES + owner_map // radix).reshape(devices, 1, items)
+    blocks = samples.reshape(2, stations, frames * radix, LANES)
+    taps = filter_taps.reshape(TAPS, radix, LANES)
+
+    def spectra(side, history, which):
+        return pl.pallas_call(
+            partial(spectra_kernel, which),
+            grid=(stations // GROUP,),
+            in_specs=[
+                pl.BlockSpec(memory_space=pltpu.SMEM),
+                pl.BlockSpec((2, GROUP, part_rows, LANES), lambda g: (0, g, side, 0)),
+                pl.BlockSpec((2, GROUP, TAPS * radix, LANES), lambda g: (0, g, 0, 0)),
+                whole(TAPS, radix, LANES),
+                whole(*w1h.shape),
+                whole(*w1l.shape),
+                whole(2, radix, LANES),
+                whole(*w2h.shape),
+                whole(*w2l.shape),
+                pl.BlockSpec((2, part_frames, GROUP, radix), lambda g: (0, side, g, 0)),
+                pl.BlockSpec((2, part_frames, GROUP, LANES), lambda g: (0, side, g, 0)),
+            ],
+            out_specs=pl.BlockSpec((2, part_frames, GROUP, channels), lambda g: (0, 0, g, 0)),
+            out_shape=jax.ShapeDtypeStruct((2, part_frames, stations, channels), jnp.bfloat16),
+            scratch_shapes=[
+                pltpu.VMEM((2, (part_frames + TAPS) * radix + 8, LANES), jnp.float32),
+                pltpu.VMEM((2, (part_frames + TAPS - 1) * radix, LANES), jnp.float32),
+                pltpu.VMEM((radix * rows, LANES), jnp.float32),
+                pltpu.VMEM((radix * rows, LANES), jnp.float32),
+            ],
+            compiler_params=pltpu.CompilerParams(vmem_limit_bytes=40 * 2**20),
+            cost_estimate=pl.CostEstimate(
+                flops=8 * 10**9, bytes_accessed=8 * 2**20, transcendentals=0
+            ),
+        )(delays, blocks, history, taps, w1h, w1l, twist, w2h, w2l, e1, e2)
+
+    lines = frames * stations
+    late = spectra(1, blocks, 0).reshape(lines, channels)
+    early = spectra(0, tail.reshape(2, stations, TAPS * radix, LANES), 1).reshape(lines, channels)
+
+    members = DUMP_SEGS
+    dump_count = devices // members
+    share = items * dump_count
+    picked = (owner_map % radix * LANES + owner_map // radix).reshape(dump_count, members, items)
+    picked = picked.transpose(1, 0, 2).reshape(members, 1, share)
     packed = pl.pallas_call(
         reorder_kernel,
-        grid=(devices,),
+        grid=(members,),
         in_specs=[
-            pl.BlockSpec((1, 1, items), lambda d: (d, 0, 0)),
+            pl.BlockSpec((1, 1, share), lambda d: (d, 0, 0)),
+            pl.BlockSpec((lines, channels), lambda d: (0, 0)),
             pl.BlockSpec((lines, channels), lambda d: (0, 0)),
         ],
-        out_specs=pl.BlockSpec((1, lines, items), lambda d: (d, 0, 0)),
-        out_shape=jax.ShapeDtypeStruct((devices, lines, items), jnp.bfloat16),
-        compiler_params=pltpu.CompilerParams(vmem_limit_bytes=40 * 2**20),
-    )(picked, rotated.reshape(lines, channels))
-
-    received = lax.all_to_all(packed, "row", split_axis=0, concat_axis=0, tiled=True)
-    received = received.reshape(devices, 2, frames, stations, items)
-    dump_count = devices // DUMP_SEGS
-    tile = min(LANES, items)
-    return pl.pallas_call(
+        out_specs=pl.BlockSpec((1, 2 * lines, share), lambda d: (d, 0, 0)),
+        out_shape=jax.ShapeDtypeStruct((members, 2 * lines, share), jnp.bfloat16),
+        compiler_params=pltpu.CompilerParams(vmem_limit_bytes=50 * 2**20),
+    )(picked, early, late)
+
+    near = [[g * members + i for i in range(members)] for g in range(dump_count)]
+    far = [[g * members + i for g in range(dump_count)] for i in range(members)]
+    received = lax.all_to_all(
+        packed, "row", split_axis=0, concat_axis=0, tiled=True, axis_index_groups=near
+    )
+    received = received.reshape(members, 2, 2, part_frames, stations, share)
+    pairs = stations * stations
+    height = pairs + stations
+    direct = items % LANES == 0
+    owners, width = (dump_count, items) if direct else (1, share)
+    per = width // LANES
+    products = pl.pallas_call(
         correlate_kernel,
-        grid=(dump_count, items // tile),
+        grid=(share // LANES,),
         in_specs=[
-            pl.BlockSpec((DUMP_SEGS, 2, frames, stations, tile), lambda g, m: (g, 0, 0, 0, m)),
+            pl.BlockSpec(
+                (members, 2, 2, part_frames, stations, LANES), lambda m: (0, 0, 0, 0, 0, m)
+            ),
         ],
-        out_specs=pl.BlockSpec((2, 1, tile, stations * stations), lambda g, m: (0, g, m, 0)),
-        out_shape=jax.ShapeDtypeStruct((2, dump_count, items, stations * stations), jnp.float32),
+        out_specs=pl.BlockSpec((1, height, LANES), lambda m: (m // per, 0, m % per)),
+        out_shape=jax.ShapeDtypeStruct((owners, height, width), jnp.bfloat16),
         scratch_shapes=[
-            pltpu.VMEM((2, DUMP_SEGS * frames, stations, tile), jnp.float32),
-            pltpu.VMEM((2, stations * stations, tile), jnp.float32),
+            pltpu.VMEM((2, members * frames, stations, LANES), jnp.float32),
+            pltpu.VMEM((2, pairs, LANES), jnp.float32),
         ],
         compiler_params=pltpu.CompilerParams(vmem_limit_bytes=40 * 2**20),
     )(received)
+    if not direct:
+        products = products.reshape(height, dump_count, items).transpose(1, 0, 2)
+    gathered = lax.all_to_all(
+        products, "row", split_axis=0, concat_axis=0, tiled=True, axis_index_groups=far
+    )
+    tile = LANES if direct else items
+    return pl.pallas_call(
+        spread_kernel,
+        grid=(dump_count, items // tile),
+        in_specs=[pl.BlockSpec((1, height, tile), lambda g, m: (g, 0, m))],
+        out_specs=pl.BlockSpec((2, 1, tile, pairs), lambda g, m: (0, g, m, 0)),
+        out_shape=jax.ShapeDtypeStruct((2, dump_count, items, pairs), jnp.float32),
+        scratch_shapes=[
+            pltpu.VMEM((height, tile), jnp.float32),
+            pltpu.VMEM((2, pairs, tile), jnp.float32),
+        ],
+        compiler_params=pltpu.CompilerParams(vmem_limit_bytes=40 * 2**20),
+    )(gathered)
 
 
 def solution(mesh):

time: 216 us -> 199 us (0.921)
  blocking collectives: 114 us -> 82.3 us
  Pallas kernels: 83 us -> 93.8 us
  local copies, waits for them, and re-layouts: 9.95 us -> 13.5 us
    all_to_all x1 -> x2, blocking collectives: 114 us -> 82.3 us  [the longest x1 52.6 us: shards(): lax.all_to_all(packed, 'row', split_axis=0, concat_axis=0, tiled=True, ax...]
    pallas_call x3 -> x5, Pallas kernels: 83 us -> 93.8 us  [the longest x2 38 us: spectra(): pl.pallas_call(partial(spectra_kernel, which), grid=(stations // GROUP,),...]
    unnamed x21 -> x23, local copies, waits for them, and re-layouts: 6.02 us -> 9.61 us
  transfers between devices with their start and end apart: 2 -> 2, of which waited for: 0 -> 0; matrix products, arithmetic and copies ran while one was open for 5% -> 5% of each run, Pallas kernels for 0% -> 10%
where the time goes in v2:
time: 199 us; the launch traced here: 198 us
  Pallas kernels  93.8 us (47%)
  blocking collectives  82.3 us (41%)
  local copies, waits for them, and re-layouts  13.5 us (7%)
  starting transfers between devices  7.13 us (4%)
    all_to_all x1, blocking collectives, shards(): lax.all_to_all(packed, 'row', split_axis=0, concat_axis=0, tiled=True, ax...  52.6 us
    pallas_call x2, Pallas kernels, spectra(): pl.pallas_call(partial(spectra_kernel, which), grid=(stations // GROUP,),...  38 us
    pallas_call x1, Pallas kernels, shards(): pl.pallas_call(correlate_kernel, grid=(share // LANES,), in_specs=[pl.Blo...  30.3 us
    all_to_all x1, blocking collectives, shards(): lax.all_to_all(products, 'row', split_axis=0, concat_axis=0, tiled=True,...  29.7 us
    pallas_call x1, Pallas kernels, shards(): pl.pallas_call(reorder_kernel, grid=(members,), in_specs=[pl.BlockSpec((1...  21.9 us
    unnamed x23, local copies, waits for them, and re-layouts  9.61 us
    ppermute x2, starting transfers between devices, shards(): lax.ppermute((samples[:, :, seg_len - tail_len:], delay_knots), 'row', ro...  7.13 us
  transfers between devices with their start and end apart: 2, of which 0 were waited for; matrix products, arithmetic and copies ran while one was open for 5% of the time, Pallas kernels for 10%

profile of v2, /device:TPU:0, one launch (start us, length us, event | category | flops | bytes accessed | tf_op | source)
XLA Modules:
  0.0 198.3 jit_solution(17440805909524537859)
XLA Ops:
  0.0 0.0 copy-start.9
  0.0 2.5 %collective-permute-start.1 = (bf16[2,32,1]{1,0,2:T(2,128)(2,1)}, bf16[2,32,1]{1,0,2:T(2,128)(2,1)S(1)}, u32[]{:S(2)}, u32[]{:S(2)}) collective-permute-start(bf16[2,32,1]{1,0,2:T(2,128)(2,1)} %param.11), channel_id=1, source_target_pairs={{0,1},{1,2},{2,3},{3,4},{4,5},{5,6},{6,7},{7,8},{8,9},{9,10},{10,1... | collective-permute-start | bytes 392 | tf_op jit(solution)/shard_map/ppermute | solution.py:228
  2.5 3.1 %slice.9 = bf16[2,32,16384]{2,1,0:T(8,128)(2,1)} slice(bf16[2,32,32768]{2,1,0:T(8,128)(2,1)} %param.10), slice={[0:2], [0:32], [16384:32768]} | slice | bytes 4194304 | tf_op jit(solution)/shard_map/slice | solution.py:228
  5.5 4.7 %collective-permute-start = (bf16[2,32,16384]{2,1,0:T(8,128)(2,1)}, bf16[2,32,16384]{2,1,0:T(8,128)(2,1)S(1)}, u32[]{:S(2)}, u32[]{:S(2)}) collective-permute-start(bf16[2,32,16384]{2,1,0:T(8,128)(2,1)} %slice.9), channel_id=1, source_target_pairs={{0,1},{1,2},{2,3},{3,4},{4,5},{5,6},{6,7},{7,8},{8,9},{9,10},{10,1... | collective-permute-start | bytes 6291464 | tf_op jit(solution)/shard_map/ppermute | solution.py:228
  10.2 0.0 copy-done.9
  10.3 0.0 copy-start.7
  10.3 0.0 copy-start.8
  10.3 0.0 copy-start.2
  10.3 0.0 copy-start.3
  10.3 0.0 copy-start.4
  10.3 0.0 copy-start.5
  10.4 0.0 copy-start.6
  10.4 5.5 %copy.12 = bf16[8,8,256,128]{3,2,1,0:T(8,128)(2,1)} copy(bf16[8,8,256,128]{3,1,2,0:T(8,128)(2,1)} %bitcast.41) | data formatting | bytes 8388608
  15.8 0.0 copy-done.7
  15.9 0.0 copy-done.8
  15.9 0.8 dynamic-slice_bitcast_fusion.1
  16.7 0.0 collective-permute-done.1
  16.8 0.1 multiply_add_fusion.1
  16.9 0.6 fusion.1
  17.5 0.5 multiply_cosine_fusion
  18.0 0.0 copy-done.2
  18.0 0.0 copy-done.3
  18.0 0.0 copy-done.4
  18.1 0.0 copy-done.5
  18.1 0.0 copy-done.6
  18.1 0.0 copy-start
  18.1 2.2 %copy-done = bf16[8,8,256,128]{3,2,1,0:T(8,128)(2,1)S(1)} copy-done((bf16[8,8,256,128]{3,2,1,0:T(8,128)(2,1)S(1)}, bf16[8,8,256,128]{3,2,1,0:T(8,128)(2,1)}, u32[]{:S(2)}) %copy-start) | copy-done | bytes 4194328
  20.3 19.0 %shard_map.101 = bf16[2,4,32,4096]{3,2,1,0:T(8,128)(2,1)S(1)} custom-call(s32[2,32]{1,0:T(2,128)S(1)} %pad_add_fusion.delays_ref, bf16[2,32,256,128]{3,2,1,0:T(8,128)(2,1)S(1)} %bitcast.33, bf16[2,32,256,128]{3,2,1,0:T(8,128)(2,1)S(1)} %bitcast.34, f32[4,32,128]{2,1,0:T(8,128)S(1)} %bitcast.39, bf16[128,128]{1,0:T(8,128)(2,1)S(1)} %copy-done.4, ...), custom_call_target="tpu_custom_call" | custom-call | flops 8000000000 | bytes 8388608 | tf_op jit(solution)/shard_map/pallas_call | solution.py:267
  39.2 0.0 copy-start.1
  39.2 1.3 copy-done.1
  40.6 0.0 collective-permute-done
  40.6 0.6 copy.13
  41.2 19.0 %shard_map.100 = bf16[2,4,32,4096]{3,2,1,0:T(8,128)(2,1)S(1)} custom-call(s32[2,32]{1,0:T(2,128)S(1)} %pad_add_fusion.delays_ref, bf16[2,32,256,128]{3,2,1,0:T(8,128)(2,1)S(1)} %bitcast.35, bf16[2,32,128,128]{3,2,1,0:T(8,128)(2,1)S(1)} %bitcast.36, f32[4,32,128]{2,1,0:T(8,128)S(1)} %bitcast.40, bf16[128,128]{1,0:T(8,128)(2,1)S(1)} %copy-done.4, ...), custom_call_target="tpu_custom_call" | custom-call | flops 8000000000 | bytes 8388608 | tf_op jit(solution)/shard_map/pallas_call | solution.py:267
  60.2 21.9 %shard_map.102 = bf16[8,512,512]{2,1,0:T(8,128)(2,1)} custom-call(s32[8,1,512]{2,1,0:T(1,128)S(1)} %reshape.96.picked_ref, bf16[256,4096]{1,0:T(8,128)(2,1)S(1)} %bitcast.38, bf16[256,4096]{1,0:T(8,128)(2,1)} %bitcast.37), custom_call_target="tpu_custom_call" | custom-call | tf_op jit(solution)/shard_map/pallas_call | solution.py:306
  82.1 52.6 %all_to_all.10 = bf16[8,512,512]{2,1,0:T(8,128)(2,1)S(1)} all-to-all(bf16[8,512,512]{2,1,0:T(8,128)(2,1)} %shard_map.102), channel_id=1, replica_groups={{0,1,2,3,4,5,6,7},{8,9,10,11,12,13,14,15},{16,17,18,19,20,21,22,23},{24..., dimensions={0} | all-to-all | bytes 8388608 | tf_op jit(solution)/shard_map/all_to_all | solution.py:321
  134.7 30.3 %shard_map.103 = bf16[2,1056,256]{2,1,0:T(8,128)(2,1)S(1)} custom-call(bf16[8,2,2,4,32,512]{5,4,3,2,1,0:T(8,128)(2,1)S(1)} %bitcast.32), custom_call_target="tpu_custom_call" | custom-call | tf_op jit(solution)/shard_map/pallas_call | solution.py:330
  165.0 29.7 %all_to_all.11.packed_ref = bf16[2,1056,256]{2,1,0:T(8,128)(2,1)S(1)} all-to-all(bf16[2,1056,256]{2,1,0:T(8,128)(2,1)S(1)} %shard_map.103), channel_id=1, replica_groups={{0,8},{1,9},{2,10},{3,11},{4,12},{5,13},{6,14},{7,15},{16,24},{17,25},{..., dimensions={0} | all-to-all | bytes 2162688 | tf_op jit(solution)/shard_map/all_to_all | solution.py:348
  194.7 3.5 %shard_map.104 = f32[2,2,256,1024]{3,2,1,0:T(8,128)} custom-call(bf16[2,1056,256]{2,1,0:T(8,128)(2,1)S(1)} %all_to_all.11.packed_ref), custom_call_target="tpu_custom_call" | custom-call | tf_op jit(solution)/shard_map/pallas_call | solution.py:352
  (14 shorter events, 0.2 us)
Async XLA Ops:
  0.0 10.2 %copy-start.9 = (bf16[2,32,1]{1,0,2:T(2,128)(2,1)S(1)}, bf16[2,32,1]{1,0,2:T(2,128)(2,1)}, u32[]{:S(2)}) copy-start(bf16[2,32,1]{1,0,2:T(2,128)(2,1)} %param.11) | copy-start | bytes 388
  0.0 16.7 %collective-permute-start.1 = (bf16[2,32,1]{1,0,2:T(2,128)(2,1)}, bf16[2,32,1]{1,0,2:T(2,128)(2,1)S(1)}, u32[]{:S(2)}, u32[]{:S(2)}) collective-permute-start(bf16[2,32,1]{1,0,2:T(2,128)(2,1)} %param.11), channel_id=1, source_target_pairs={{0,1},{1,2},{2,3},{3,4},{4,5},{5,6},{6,7},{7,8},{8,9},{9,10},{10,1... | collective-permute-start | bytes 392 | tf_op jit(solution)/shard_map/ppermute | solution.py:228
  5.5 35.0 %collective-permute-start = (bf16[2,32,16384]{2,1,0:T(8,128)(2,1)}, bf16[2,32,16384]{2,1,0:T(8,128)(2,1)S(1)}, u32[]{:S(2)}, u32[]{:S(2)}) collective-permute-start(bf16[2,32,16384]{2,1,0:T(8,128)(2,1)} %slice.9), channel_id=1, source_target_pairs={{0,1},{1,2},{2,3},{3,4},{4,5},{5,6},{6,7},{7,8},{8,9},{9,10},{10,1... | collective-permute-start | bytes 6291464 | tf_op jit(solution)/shard_map/ppermute | solution.py:228
  10.3 5.6 %copy-start.7 = (f32[4,4096]{1,0:T(4,128)S(1)}, f32[4,4096]{1,0:T(4,128)}, u32[]{:S(2)}) copy-start(f32[4,4096]{1,0:T(4,128)} %param.14) | copy-start | bytes 196612
  10.3 5.6 %copy-start.8 = (s32[4096]{0:T(1024)S(1)}, s32[4096]{0:T(1024)}, u32[]{:S(2)}) copy-start(s32[4096]{0:T(1024)} %param.13) | copy-start | bytes 49156
  10.3 7.7 %copy-start.2 = (bf16[256,256]{1,0:T(8,128)(2,1)S(1)}, bf16[256,256]{1,0:T(8,128)(2,1)}, u32[]{:S(2)}) copy-start(bf16[256,256]{1,0:T(8,128)(2,1)} %constant.76.clone.w2h_ref) | copy-start | bytes 393220
  10.3 7.7 %copy-start.3 = (bf16[256,256]{1,0:T(8,128)(2,1)S(1)}, bf16[256,256]{1,0:T(8,128)(2,1)}, u32[]{:S(2)}) copy-start(bf16[256,256]{1,0:T(8,128)(2,1)} %constant.77.clone.w2l_ref) | copy-start | bytes 393220
  10.3 7.7 %copy-start.4 = (bf16[128,128]{1,0:T(8,128)(2,1)S(1)}, bf16[128,128]{1,0:T(8,128)(2,1)}, u32[]{:S(2)}) copy-start(bf16[128,128]{1,0:T(8,128)(2,1)} %constant.73.clone.w1h_ref) | copy-start | bytes 98308
  10.3 7.7 %copy-start.5 = (bf16[128,128]{1,0:T(8,128)(2,1)S(1)}, bf16[128,128]{1,0:T(8,128)(2,1)}, u32[]{:S(2)}) copy-start(bf16[128,128]{1,0:T(8,128)(2,1)} %constant.74.clone.w1l_ref) | copy-start | bytes 98308
  10.4 7.7 %copy-start.6 = (f32[2,32,128]{2,1,0:T(8,128)S(1)}, f32[2,32,128]{2,1,0:T(8,128)}, u32[]{:S(2)}) copy-start(f32[2,32,128]{2,1,0:T(8,128)} %constant.75.clone.twist_ref) | copy-start | bytes 98308
  18.1 2.2 %copy-start = (bf16[8,8,256,128]{3,2,1,0:T(8,128)(2,1)S(1)}, bf16[8,8,256,128]{3,2,1,0:T(8,128)(2,1)}, u32[]{:S(2)}) copy-start(bf16[8,8,256,128]{3,2,1,0:T(8,128)(2,1)} %copy.12) | copy-start | bytes 12582916
  39.2 1.3 copy-start.1

commit v3 on v2

--- a/solution.py
+++ b/solution.py
@@ -187,7 +187,7 @@
     out_ref[0, pairs:, :] = split_bf16(diagonal)[1]
 
 
-def spread_kernel(packed_ref, out_ref, packed, acc):
+def spread_kernel(own_ref, packed_ref, out_ref, packed, acc):
     tile = packed_ref.shape[2]
     pairs = acc.shape[1]
     stations = packed_ref.shape[1] - pairs
@@ -302,6 +302,8 @@
     dump_count = devices // members
     share = items * dump_count
     picked = (owner_map % radix * LANES + owner_map // radix).reshape(dump_count, members, items)
+    mine = position // members
+    picked = jnp.roll(picked, -mine, axis=0)
     picked = picked.transpose(1, 0, 2).reshape(members, 1, share)
     packed = pl.pallas_call(
         reorder_kernel,
@@ -317,7 +319,6 @@
     )(picked, early, late)
 
     near = [[g * members + i for i in range(members)] for g in range(dump_count)]
-    far = [[g * members + i for g in range(dump_count)] for i in range(members)]
     received = lax.all_to_all(
         packed, "row", split_axis=0, concat_axis=0, tiled=True, axis_index_groups=near
     )
@@ -325,42 +326,63 @@
     pairs = stations * stations
     height = pairs + stations
     direct = items % LANES == 0
-    owners, width = (dump_count, items) if direct else (1, share)
+    width = items if direct else share
     per = width // LANES
-    products = pl.pallas_call(
-        correlate_kernel,
-        grid=(share // LANES,),
-        in_specs=[
-            pl.BlockSpec(
-                (members, 2, 2, part_frames, stations, LANES), lambda m: (0, 0, 0, 0, 0, m)
+
+    def correlate(first):
+        return pl.pallas_call(
+            correlate_kernel,
+            grid=(per,),
+            in_specs=[
+                pl.BlockSpec(
+                    (members, 2, 2, part_frames, stations, LANES),
+                    lambda m: (0, 0, 0, 0, 0, first + m),
+                ),
+            ],
+            out_specs=pl.BlockSpec((1, height, LANES), lambda m: (0, 0, m)),
+            out_shape=jax.ShapeDtypeStruct((1, height, width), jnp.bfloat16),
+            scratch_shapes=[
+                pltpu.VMEM((2, members * frames, stations, LANES), jnp.float32),
+                pltpu.VMEM((2, pairs, LANES), jnp.float32),
+            ],
+            compiler_params=pltpu.CompilerParams(vmem_limit_bytes=40 * 2**20),
+            cost_estimate=pl.CostEstimate(
+                flops=8 * 10**9, bytes_accessed=8 * 2**20, transcendentals=0
             ),
-        ],
-        out_specs=pl.BlockSpec((1, height, LANES), lambda m: (m // per, 0, m % per)),
-        out_shape=jax.ShapeDtypeStruct((owners, height, width), jnp.bfloat16),
-        scratch_shapes=[
-            pltpu.VMEM((2, members * frames, stations, LANES), jnp.float32),
-            pltpu.VMEM((2, pairs, LANES), jnp.float32),
-        ],
-        compiler_params=pltpu.CompilerParams(vmem_limit_bytes=40 * 2**20),
-    )(received)
+        )(received)
+
     if not direct:
-        products = products.reshape(height, dump_count, items).transpose(1, 0, 2)
-    gathered = lax.all_to_all(
-        products, "row", split_axis=0, concat_axis=0, tiled=True, axis_index_groups=far
-    )
+        everything = correlate(0)
+    gathered = [None] * dump_count
+    for k in list(range(1, dump_count)) + [0]:
+        if direct:
+            product = correlate(k * per)
+        else:
+            product = everything[:, :, k * items : (k + 1) * items]
+        if k:
+            route = [(i, (i + k * members) % devices) for i in range(devices)]
+            product = lax.ppermute(product, "row", route)
+        gathered[k] = product
+    gathered = jnp.concatenate(gathered, axis=0)
     tile = LANES if direct else items
     return pl.pallas_call(
         spread_kernel,
-        grid=(dump_count, items // tile),
-        in_specs=[pl.BlockSpec((1, height, tile), lambda g, m: (g, 0, m))],
-        out_specs=pl.BlockSpec((2, 1, tile, pairs), lambda g, m: (0, g, m, 0)),
+        grid_spec=pltpu.PrefetchScalarGridSpec(
+            num_scalar_prefetch=1,
+            grid=(dump_count, items // tile),
+            in_specs=[pl.BlockSpec((1, height, tile), lambda k, m, own: (k, 0, m))],
+            out_specs=pl.BlockSpec(
+                (2, 1, tile, pairs),
+                lambda k, m, own: (0, lax.rem(own[0] + dump_count - k, dump_count), m, 0),
+            ),
+            scratch_shapes=[
+                pltpu.VMEM((height, tile), jnp.float32),
+                pltpu.VMEM((2, pairs, tile), jnp.float32),
+            ],
+        ),
         out_shape=jax.ShapeDtypeStruct((2, dump_count, items, pairs), jnp.float32),
-        scratch_shapes=[
-            pltpu.VMEM((height, tile), jnp.float32),
-            pltpu.VMEM((2, pairs, tile), jnp.float32),
-        ],
         compiler_params=pltpu.CompilerParams(vmem_limit_bytes=40 * 2**20),
-    )(gathered)
+    )(jnp.full((1,), mine, jnp.int32), gathered)
 
 
 def solution(mesh):

time: 199 us -> 180 us (0.905)
  blocking collectives: 82.3 us -> 52.6 us
  waiting for transfers between devices: 0.01 us -> 8.98 us
  starting transfers between devices: 7.13 us -> 9.51 us
    all_to_all x1 -> x0, blocking collectives: 29.7 us -> none  [shards(): lax.all_to_all(products, 'row', split_axis=0, concat_axis=0, tiled=True,...]
    ppermute x0 -> x1, waiting for transfers between devices: none -> 8.98 us  [shards(): product = lax.ppermute(product, 'row', route)]
    ppermute x0 -> x1, starting transfers between devices: none -> 2.37 us  [shards(): product = lax.ppermute(product, 'row', route)]
    pallas_call x2 -> x3, Pallas kernels: 33.8 us -> 33.9 us  [the longest x2 30.3 us: correlate(): pl.pallas_call(correlate_kernel, grid=(per,), in_specs=[pl.BlockSpec((mem...]
  transfers between devices with their start and end apart: 2 -> 3, of which waited for: 0 -> 1; matrix products, arithmetic and copies ran while one was open for 5% -> 6% of each run, Pallas kernels for 10% -> 19%
where the time goes in v3:
time: 180 us
  Pallas kernels  93.8 us (52%)
  blocking collectives  52.6 us (29%)
  local copies, waits for them, and re-layouts  13.5 us (8%)
  starting transfers between devices  9.51 us (5%)
  waiting for transfers between devices  8.98 us (5%)
    all_to_all x1, blocking collectives, shards(): lax.all_to_all(packed, 'row', split_axis=0, concat_axis=0, tiled=True, ax...  52.6 us
    pallas_call x2, Pallas kernels, spectra(): pl.pallas_call(partial(spectra_kernel, which), grid=(stations // GROUP,),...  38 us
    pallas_call x2, Pallas kernels, correlate(): pl.pallas_call(correlate_kernel, grid=(per,), in_specs=[pl.BlockSpec((mem...  30.3 us
    pallas_call x1, Pallas kernels, shards(): pl.pallas_call(reorder_kernel, grid=(members,), in_specs=[pl.BlockSpec((1...  21.9 us
    unnamed x23, local copies, waits for them, and re-layouts  9.6 us
    ppermute x1, waiting for transfers between devices, shards(): product = lax.ppermute(product, 'row', route)  8.98 us
    ppermute x2, starting transfers between devices, shards(): lax.ppermute((samples[:, :, seg_len - tail_len:], delay_knots), 'row', ro...  7.13 us
  transfers between devices with their start and end apart: 3, of which 1 were waited for; matrix products, arithmetic and copies ran while one was open for 6% of the time, Pallas kernels for 19%

profile of v3, /device:TPU:0, one launch (start us, length us, event | category | flops | bytes accessed | tf_op | source)
XLA Modules:
  0.0 180.1 jit_solution(10329558491934187298)
XLA Ops:
  0.0 0.0 copy-start.9
  0.0 2.5 %collective-permute-start.1 = (bf16[2,32,1]{1,0,2:T(2,128)(2,1)}, bf16[2,32,1]{1,0,2:T(2,128)(2,1)S(1)}, u32[]{:S(2)}, u32[]{:S(2)}) collective-permute-start(bf16[2,32,1]{1,0,2:T(2,128)(2,1)} %param.11), channel_id=1, source_target_pairs={{0,1},{1,2},{2,3},{3,4},{4,5},{5,6},{6,7},{7,8},{8,9},{9,10},{10,1... | collective-permute-start | bytes 392 | tf_op jit(solution)/shard_map/ppermute | solution.py:228
  2.5 3.1 %slice.9 = bf16[2,32,16384]{2,1,0:T(8,128)(2,1)} slice(bf16[2,32,32768]{2,1,0:T(8,128)(2,1)} %param.10), slice={[0:2], [0:32], [16384:32768]} | slice | bytes 4194304 | tf_op jit(solution)/shard_map/slice | solution.py:228
  5.6 4.7 %collective-permute-start = (bf16[2,32,16384]{2,1,0:T(8,128)(2,1)}, bf16[2,32,16384]{2,1,0:T(8,128)(2,1)S(1)}, u32[]{:S(2)}, u32[]{:S(2)}) collective-permute-start(bf16[2,32,16384]{2,1,0:T(8,128)(2,1)} %slice.9), channel_id=1, source_target_pairs={{0,1},{1,2},{2,3},{3,4},{4,5},{5,6},{6,7},{7,8},{8,9},{9,10},{10,1... | collective-permute-start | bytes 6291464 | tf_op jit(solution)/shard_map/ppermute | solution.py:228
  10.2 0.0 copy-done.9
  10.3 0.0 copy-start.7
  10.3 0.0 copy-start.8
  10.3 0.0 copy-start.2
  10.4 0.0 copy-start.3
  10.4 0.0 copy-start.4
  10.4 0.0 copy-start.5
  10.4 0.0 copy-start.6
  10.4 5.5 %copy.12 = bf16[8,8,256,128]{3,2,1,0:T(8,128)(2,1)} copy(bf16[8,8,256,128]{3,1,2,0:T(8,128)(2,1)} %bitcast.44) | data formatting | bytes 8388608
  15.9 0.0 copy-done.7
  15.9 0.0 copy-done.8
  16.0 0.8 fusion.11
  16.8 0.0 collective-permute-done.1
  16.9 0.1 multiply_add_fusion.1
  16.9 0.6 fusion.1
  17.5 0.5 multiply_cosine_fusion
  18.1 0.0 copy-done.2
  18.1 0.0 copy-done.3
  18.1 0.0 copy-done.4
  18.1 0.0 copy-done.5
  18.1 0.0 copy-done.6
  18.2 0.0 copy-start
  18.2 2.2 %copy-done = bf16[8,8,256,128]{3,2,1,0:T(8,128)(2,1)S(1)} copy-done((bf16[8,8,256,128]{3,2,1,0:T(8,128)(2,1)S(1)}, bf16[8,8,256,128]{3,2,1,0:T(8,128)(2,1)}, u32[]{:S(2)}) %copy-start) | copy-done | bytes 4194328
  20.3 19.0 %shard_map.101 = bf16[2,4,32,4096]{3,2,1,0:T(8,128)(2,1)S(1)} custom-call(s32[2,32]{1,0:T(2,128)S(1)} %pad_add_fusion.delays_ref, bf16[2,32,256,128]{3,2,1,0:T(8,128)(2,1)S(1)} %bitcast.34, bf16[2,32,256,128]{3,2,1,0:T(8,128)(2,1)S(1)} %bitcast.35, f32[4,32,128]{2,1,0:T(8,128)S(1)} %bitcast.42, bf16[128,128]{1,0:T(8,128)(2,1)S(1)} %copy-done.4, ...), custom_call_target="tpu_custom_call" | custom-call | flops 8000000000 | bytes 8388608 | tf_op jit(solution)/shard_map/pallas_call | solution.py:267
  39.3 0.0 copy-start.1
  39.3 1.3 copy-done.1
  40.6 0.0 collective-permute-done
  40.6 0.6 copy.13
  41.2 19.0 %shard_map.100 = bf16[2,4,32,4096]{3,2,1,0:T(8,128)(2,1)S(1)} custom-call(s32[2,32]{1,0:T(2,128)S(1)} %pad_add_fusion.delays_ref, bf16[2,32,256,128]{3,2,1,0:T(8,128)(2,1)S(1)} %bitcast.36, bf16[2,32,128,128]{3,2,1,0:T(8,128)(2,1)S(1)} %bitcast.39, f32[4,32,128]{2,1,0:T(8,128)S(1)} %bitcast.43, bf16[128,128]{1,0:T(8,128)(2,1)S(1)} %copy-done.4, ...), custom_call_target="tpu_custom_call" | custom-call | flops 8000000000 | bytes 8388608 | tf_op jit(solution)/shard_map/pallas_call | solution.py:267
  60.2 21.9 %shard_map.102 = bf16[8,512,512]{2,1,0:T(8,128)(2,1)} custom-call(s32[8,1,512]{2,1,0:T(1,128)S(1)} %reshape.96.picked_ref, bf16[256,4096]{1,0:T(8,128)(2,1)S(1)} %bitcast.41, bf16[256,4096]{1,0:T(8,128)(2,1)} %bitcast.40), custom_call_target="tpu_custom_call" | custom-call | tf_op jit(solution)/shard_map/pallas_call | solution.py:308
  82.2 52.6 %all_to_all.5 = bf16[8,512,512]{2,1,0:T(8,128)(2,1)S(1)} all-to-all(bf16[8,512,512]{2,1,0:T(8,128)(2,1)} %shard_map.102), channel_id=1, replica_groups={{0,1,2,3,4,5,6,7},{8,9,10,11,12,13,14,15},{16,17,18,19,20,21,22,23},{24..., dimensions={0} | all-to-all | bytes 8388608 | tf_op jit(solution)/shard_map/all_to_all | solution.py:322
  134.8 15.1 %shard_map.104 = bf16[1,1056,256]{2,1,0:T(8,128)(2,1)S(1)} custom-call(bf16[8,2,2,4,32,512]{5,4,3,2,1,0:T(8,128)(2,1)S(1)} %bitcast.37), custom_call_target="tpu_custom_call" | custom-call | flops 8000000000 | bytes 8388608 | tf_op jit(solution)/shard_map/pallas_call | solution.py:333
  149.9 2.4 %collective-permute-start.2 = (bf16[1,1056,256]{2,1,0:T(8,128)(2,1)S(1)}, bf16[1,1056,256]{2,1,0:T(8,128)(2,1)S(1)}, u32[]{:S(2)}, u32[]{:S(2)}) collective-permute-start(bf16[1,1056,256]{2,1,0:T(8,128)(2,1)S(1)} %shard_map.104), channel_id=1, source_target_pairs={{0,8},{1,9},{2,10},{3,11},{4,12},{5,13},{6,14},{7,15},{8,0},{9,1},... | collective-permute-start | bytes 1622024 | tf_op jit(solution)/shard_map/ppermute | solution.py:364
  152.3 15.1 %shard_map.103 = bf16[1,1056,256]{2,1,0:T(8,128)(2,1)S(1)} custom-call(bf16[8,2,2,4,32,512]{5,4,3,2,1,0:T(8,128)(2,1)S(1)} %bitcast.38), custom_call_target="tpu_custom_call" | custom-call | flops 8000000000 | bytes 8388608 | tf_op jit(solution)/shard_map/pallas_call | solution.py:333
  167.4 9.0 %collective-permute-done.2 = bf16[1,1056,256]{2,1,0:T(8,128)(2,1)S(1)} collective-permute-done((bf16[1,1056,256]{2,1,0:T(8,128)(2,1)S(1)}, bf16[1,1056,256]{2,1,0:T(8,128)(2,1)S(1)}, u32[]{:S(2)}, u32[]{:S(2)}) %collective-permute-start.2) | collective-permute-done | bytes 540704 | tf_op jit(solution)/shard_map/ppermute | solution.py:364
  176.4 0.1 pad_maximum_fusion.packed_ref
  176.5 3.6 %shard_map.105 = f32[2,2,256,1024]{3,2,1,0:T(8,128)} custom-call(s32[1]{0:T(128)} %bitcast.own_ref, bf16[2,1056,256]{2,1,0:T(8,128)(2,1)S(1)} %pad_maximum_fusion.packed_ref), custom_call_target="tpu_custom_call" | custom-call | tf_op jit(solution)/shard_map/pallas_call | solution.py:368
  (15 shorter events, 0.2 us)
Async XLA Ops:
  0.0 10.2 %copy-start.9 = (bf16[2,32,1]{1,0,2:T(2,128)(2,1)S(1)}, bf16[2,32,1]{1,0,2:T(2,128)(2,1)}, u32[]{:S(2)}) copy-start(bf16[2,32,1]{1,0,2:T(2,128)(2,1)} %param.11) | copy-start | bytes 388
  0.0 16.8 %collective-permute-start.1 = (bf16[2,32,1]{1,0,2:T(2,128)(2,1)}, bf16[2,32,1]{1,0,2:T(2,128)(2,1)S(1)}, u32[]{:S(2)}, u32[]{:S(2)}) collective-permute-start(bf16[2,32,1]{1,0,2:T(2,128)(2,1)} %param.11), channel_id=1, source_target_pairs={{0,1},{1,2},{2,3},{3,4},{4,5},{5,6},{6,7},{7,8},{8,9},{9,10},{10,1... | collective-permute-start | bytes 392 | tf_op jit(solution)/shard_map/ppermute | solution.py:228
  5.6 35.1 %collective-permute-start = (bf16[2,32,16384]{2,1,0:T(8,128)(2,1)}, bf16[2,32,16384]{2,1,0:T(8,128)(2,1)S(1)}, u32[]{:S(2)}, u32[]{:S(2)}) collective-permute-start(bf16[2,32,16384]{2,1,0:T(8,128)(2,1)} %slice.9), channel_id=1, source_target_pairs={{0,1},{1,2},{2,3},{3,4},{4,5},{5,6},{6,7},{7,8},{8,9},{9,10},{10,1... | collective-permute-start | bytes 6291464 | tf_op jit(solution)/shard_map/ppermute | solution.py:228
  10.3 5.6 %copy-start.7 = (f32[4,4096]{1,0:T(4,128)S(1)}, f32[4,4096]{1,0:T(4,128)}, u32[]{:S(2)}) copy-start(f32[4,4096]{1,0:T(4,128)} %param.14) | copy-start | bytes 196612
  10.3 5.6 %copy-start.8 = (s32[4096]{0:T(1024)S(1)}, s32[4096]{0:T(1024)}, u32[]{:S(2)}) copy-start(s32[4096]{0:T(1024)} %param.13) | copy-start | bytes 49156
  10.3 7.8 %copy-start.2 = (bf16[256,256]{1,0:T(8,128)(2,1)S(1)}, bf16[256,256]{1,0:T(8,128)(2,1)}, u32[]{:S(2)}) copy-start(bf16[256,256]{1,0:T(8,128)(2,1)} %constant.109.clone.w2h_ref) | copy-start | bytes 393220
  10.4 7.8 %copy-start.3 = (bf16[256,256]{1,0:T(8,128)(2,1)S(1)}, bf16[256,256]{1,0:T(8,128)(2,1)}, u32[]{:S(2)}) copy-start(bf16[256,256]{1,0:T(8,128)(2,1)} %constant.110.clone.w2l_ref) | copy-start | bytes 393220
  10.4 7.8 %copy-start.4 = (bf16[128,128]{1,0:T(8,128)(2,1)S(1)}, bf16[128,128]{1,0:T(8,128)(2,1)}, u32[]{:S(2)}) copy-start(bf16[128,128]{1,0:T(8,128)(2,1)} %constant.106.clone.w1h_ref) | copy-start | bytes 98308
  10.4 7.8 %copy-start.5 = (bf16[128,128]{1,0:T(8,128)(2,1)S(1)}, bf16[128,128]{1,0:T(8,128)(2,1)}, u32[]{:S(2)}) copy-start(bf16[128,128]{1,0:T(8,128)(2,1)} %constant.107.clone.w1l_ref) | copy-start | bytes 98308
  10.4 7.7 %copy-start.6 = (f32[2,32,128]{2,1,0:T(8,128)S(1)}, f32[2,32,128]{2,1,0:T(8,128)}, u32[]{:S(2)}) copy-start(f32[2,32,128]{2,1,0:T(8,128)} %constant.108.clone.twist_ref) | copy-start | bytes 98308
  18.2 2.2 %copy-start = (bf16[8,8,256,128]{3,2,1,0:T(8,128)(2,1)S(1)}, bf16[8,8,256,128]{3,2,1,0:T(8,128)(2,1)}, u32[]{:S(2)}) copy-start(bf16[8,8,256,128]{3,2,1,0:T(8,128)(2,1)} %copy.12) | copy-start | bytes 12582916
  39.3 1.3 copy-start.1
  149.9 26.5 %collective-permute-start.2 = (bf16[1,1056,256]{2,1,0:T(8,128)(2,1)S(1)}, bf16[1,1056,256]{2,1,0:T(8,128)(2,1)S(1)}, u32[]{:S(2)}, u32[]{:S(2)}) collective-permute-start(bf16[1,1056,256]{2,1,0:T(8,128)(2,1)S(1)} %shard_map.104), channel_id=1, source_target_pairs={{0,8},{1,9},{2,10},{3,11},{4,12},{5,13},{6,14},{7,15},{8,0},{9,1},... | collective-permute-start | bytes 1622024 | tf_op jit(solution)/shard_map/ppermute | solution.py:364

commit v4 on v3

--- a/solution.py
+++ b/solution.py
@@ -14,6 +14,7 @@
 LANES = 128
 GROUP = 8
 SUB = 8
+ROWS = 4
 
 
 def block_matrix(size, scale):
@@ -48,23 +49,24 @@
     base = pl.program_id(0) * GROUP
     lane = lax.broadcasted_iota(jnp.int32, (1, LANES), 1)
 
-    def shift(part, start, count, where):
+    def shift(spare, part, start, count, where):
         row = start // LANES
         turn = start % LANES
         back = (LANES - turn) % LANES
-        near = pltpu.roll(window[part, pl.ds(row, count), :], back, 1)
-        far = pltpu.roll(window[part, pl.ds(row + 1, count), :], back, 1)
-        ext[part, pl.ds(where, count), :] = jnp.where(lane < LANES - turn, near, far)
-
-    def station(index, carry):
+        near = pltpu.roll(window[spare + part, pl.ds(row, count), :], back, 1)
+        far = pltpu.roll(window[spare + part, pl.ds(row + 1, count), :], back, 1)
+        ext[spare + part, pl.ds(where, count), :] = jnp.where(lane < LANES - turn, near, far)
+
+    def station(index, spare):
         own_delay = delays_ref[0, base + index]
         prev_delay = delays_ref[which, base + index]
         for part in range(2):
-            window[part, 0:tail_rows, :] = tail_ref[part, index].astype(jnp.float32)
-            window[part, tail_rows : tail_rows + own_rows, :] = own_ref[part, index].astype(jnp.float32)
-            shift(part, radix * LANES - prev_delay, history * radix, 0)
+            window[spare + part, 0:tail_rows, :] = tail_ref[part, index].astype(jnp.float32)
+            window[spare + part, tail_rows : tail_rows + own_rows, :] = own_ref[part, index].astype(jnp.float32)
+            shift(spare, part, radix * LANES - prev_delay, history * radix, 0)
             for frame in range(0, frames, 2):
                 shift(
+                    spare,
                     part,
                     tail_rows * LANES - own_delay + frame * radix * LANES,
                     2 * radix,
@@ -72,10 +74,10 @@
                 )
 
         def filtered(part, frame):
-            total = taps_ref[0] * ext[part, frame * radix : (frame + 1) * radix, :]
+            total = taps_ref[0] * ext[spare + part, frame * radix : (frame + 1) * radix, :]
             for tap in range(1, TAPS):
                 spot = (frame + tap) * radix
-                total = total + taps_ref[tap] * ext[part, spot : spot + radix, :]
+                total = total + taps_ref[tap] * ext[spare + part, spot : spot + radix, :]
             return total
 
         columns = []
@@ -95,10 +97,14 @@
                 place = pl.ds((side * half + f) * GROUP + index, radix, stride=rows)
                 turned_re[place, :] = real * twist_ref[0] - imag * twist_ref[1]
                 turned_im[place, :] = real * twist_ref[1] + imag * twist_ref[0]
+
+    def two_stations(pair, carry):
+        station(2 * pair, 0)
+        station(2 * pair + 1, 2)
         return carry
 
-    lax.fori_loop(0, GROUP, station, 0)
-    batch = 8
+    lax.fori_loop(0, GROUP // 2, two_stations, 0)
+    batch = 16
     e2_cos = e2_ref[0].reshape(rows, LANES)
     e2_sin = e2_ref[1].reshape(rows, LANES)
     e1_cos = e1_ref[0].reshape(rows, radix)
@@ -151,7 +157,7 @@
         width = stations - low
 
         def one_row(pair, carry):
-            mine = [low + 2 * pair, low + 2 * pair + 1]
+            mine = [low + ROWS * pair + i for i in range(ROWS)]
 
             def frame_step(f, sums):
                 b_re = data[0, f, low:, :]
@@ -165,14 +171,14 @@
                 return tuple(result)
 
             zero = jnp.zeros((width, tile), jnp.float32)
-            sums = lax.fori_loop(0, count, frame_step, (zero,) * 4, unroll=4)
+            sums = lax.fori_loop(0, count, frame_step, (zero,) * (2 * ROWS), unroll=4)
             for slot, a in enumerate(mine):
                 place = pl.ds(pl.multiple_of(a * stations + low, 8), width)
                 acc[0, place, :] = sums[2 * slot] * scale
                 acc[1, place, :] = sums[2 * slot + 1] * scale
             return carry
 
-        lax.fori_loop(0, SUB // 2, one_row, 0)
+        lax.fori_loop(0, SUB // ROWS, one_row, 0)
     diagonal = acc[0, pl.ds(0, stations, stride=stations + 1), :]
     line = lax.broadcasted_iota(jnp.int32, (SUB, tile), 0)
     for a in range(stations):
@@ -283,8 +289,8 @@
             out_specs=pl.BlockSpec((2, part_frames, GROUP, channels), lambda g: (0, 0, g, 0)),
             out_shape=jax.ShapeDtypeStruct((2, part_frames, stations, channels), jnp.bfloat16),
             scratch_shapes=[
-                pltpu.VMEM((2, (part_frames + TAPS) * radix + 8, LANES), jnp.float32),
-                pltpu.VMEM((2, (part_frames + TAPS - 1) * radix, LANES), jnp.float32),
+                pltpu.VMEM((4, (part_frames + TAPS) * radix + 8, LANES), jnp.float32),
+                pltpu.VMEM((4, (part_frames + TAPS - 1) * radix, LANES), jnp.float32),
                 pltpu.VMEM((radix * rows, LANES), jnp.float32),
                 pltpu.VMEM((radix * rows, LANES), jnp.float32),
             ],

time: 180 us -> 174 us (0.967)
  Pallas kernels: 93.8 us -> 86 us
    pallas_call x2, Pallas kernels: 38 us -> 32.6 us  [spectra(): pl.pallas_call(partial(spectra_kernel, which), grid=(stations // GROUP,),...]
    pallas_call x2, Pallas kernels: 30.3 us -> 27.9 us  [correlate(): pl.pallas_call(correlate_kernel, grid=(per,), in_specs=[pl.BlockSpec((mem...]
  transfers between devices with their start and end apart: 3 -> 3, of which waited for: 1 -> 1; matrix products, arithmetic and copies ran while one was open for 6% -> 6% of each run, Pallas kernels for 19% -> 17%
where the time goes in v4:
time: 174 us
  Pallas kernels  86 us (49%)
  blocking collectives  52.6 us (30%)
  local copies, waits for them, and re-layouts  13.5 us (8%)
  waiting for transfers between devices  10.2 us (6%)
  starting transfers between devices  9.48 us (5%)
    all_to_all x1, blocking collectives, shards(): lax.all_to_all(packed, 'row', split_axis=0, concat_axis=0, tiled=True, ax...  52.6 us
    pallas_call x2, Pallas kernels, spectra(): pl.pallas_call(partial(spectra_kernel, which), grid=(stations // GROUP,),...  32.6 us
    pallas_call x2, Pallas kernels, correlate(): pl.pallas_call(correlate_kernel, grid=(per,), in_specs=[pl.BlockSpec((mem...  27.9 us
    pallas_call x1, Pallas kernels, shards(): pl.pallas_call(reorder_kernel, grid=(members,), in_specs=[pl.BlockSpec((1...  21.9 us
    ppermute x1, waiting for transfers between devices, shards(): product = lax.ppermute(product, 'row', route)  10.2 us
    unnamed x23, local copies, waits for them, and re-layouts  9.6 us
    ppermute x2, starting transfers between devices, shards(): lax.ppermute((samples[:, :, seg_len - tail_len:], delay_knots), 'row', ro...  7.13 us
    pallas_call x1, Pallas kernels, shards(): pl.pallas_call(spread_kernel, grid_spec=pltpu.PrefetchScalarGridSpec(num_...  3.59 us
  transfers between devices with their start and end apart: 3, of which 1 were waited for; matrix products, arithmetic and copies ran while one was open for 6% of the time, Pallas kernels for 17%

profile of v4, /device:TPU:0, one launch (start us, length us, event | category | flops | bytes accessed | tf_op | source)
XLA Modules:
  0.0 173.6 jit_solution(18145170751632465414)
XLA Ops:
  0.0 0.0 copy-start.9
  0.0 2.5 %collective-permute-start.1 = (bf16[2,32,1]{1,0,2:T(2,128)(2,1)}, bf16[2,32,1]{1,0,2:T(2,128)(2,1)S(1)}, u32[]{:S(2)}, u32[]{:S(2)}) collective-permute-start(bf16[2,32,1]{1,0,2:T(2,128)(2,1)} %param.11), channel_id=1, source_target_pairs={{0,1},{1,2},{2,3},{3,4},{4,5},{5,6},{6,7},{7,8},{8,9},{9,10},{10,1... | collective-permute-start | bytes 392 | tf_op jit(solution)/shard_map/ppermute | solution.py:234
  2.5 3.1 %slice.9 = bf16[2,32,16384]{2,1,0:T(8,128)(2,1)} slice(bf16[2,32,32768]{2,1,0:T(8,128)(2,1)} %param.10), slice={[0:2], [0:32], [16384:32768]} | slice | bytes 4194304 | tf_op jit(solution)/shard_map/slice | solution.py:234
  5.6 4.7 %collective-permute-start = (bf16[2,32,16384]{2,1,0:T(8,128)(2,1)}, bf16[2,32,16384]{2,1,0:T(8,128)(2,1)S(1)}, u32[]{:S(2)}, u32[]{:S(2)}) collective-permute-start(bf16[2,32,16384]{2,1,0:T(8,128)(2,1)} %slice.9), channel_id=1, source_target_pairs={{0,1},{1,2},{2,3},{3,4},{4,5},{5,6},{6,7},{7,8},{8,9},{9,10},{10,1... | collective-permute-start | bytes 6291464 | tf_op jit(solution)/shard_map/ppermute | solution.py:234
  10.2 0.0 copy-done.9
  10.3 0.0 copy-start.7
  10.3 0.0 copy-start.8
  10.3 0.0 copy-start.2
  10.4 0.0 copy-start.3
  10.4 0.0 copy-start.4
  10.4 0.0 copy-start.5
  10.4 0.0 copy-start.6
  10.4 5.5 %copy.12 = bf16[8,8,256,128]{3,2,1,0:T(8,128)(2,1)} copy(bf16[8,8,256,128]{3,1,2,0:T(8,128)(2,1)} %bitcast.44) | data formatting | bytes 8388608
  15.9 0.0 copy-done.7
  15.9 0.0 copy-done.8
  16.0 0.8 fusion.11
  16.8 0.0 collective-permute-done.1
  16.9 0.1 multiply_add_fusion.1
  16.9 0.6 fusion.1
  17.5 0.5 multiply_cosine_fusion
  18.1 0.0 copy-done.2
  18.1 0.0 copy-done.3
  18.1 0.0 copy-done.4
  18.1 0.0 copy-done.5
  18.1 0.0 copy-done.6
  18.2 0.0 copy-start
  18.2 2.2 %copy-done = bf16[8,8,256,128]{3,2,1,0:T(8,128)(2,1)S(1)} copy-done((bf16[8,8,256,128]{3,2,1,0:T(8,128)(2,1)S(1)}, bf16[8,8,256,128]{3,2,1,0:T(8,128)(2,1)}, u32[]{:S(2)}) %copy-start) | copy-done | bytes 4194328
  20.3 16.3 %shard_map.101 = bf16[2,4,32,4096]{3,2,1,0:T(8,128)(2,1)S(1)} custom-call(s32[2,32]{1,0:T(2,128)S(1)} %pad_add_fusion.delays_ref, bf16[2,32,256,128]{3,2,1,0:T(8,128)(2,1)S(1)} %bitcast.34, bf16[2,32,256,128]{3,2,1,0:T(8,128)(2,1)S(1)} %bitcast.35, f32[4,32,128]{2,1,0:T(8,128)S(1)} %bitcast.42, bf16[128,128]{1,0:T(8,128)(2,1)S(1)} %copy-done.4, ...), custom_call_target="tpu_custom_call" | custom-call | flops 8000000000 | bytes 8388608 | tf_op jit(solution)/shard_map/pallas_call | solution.py:273
  36.6 0.0 copy-start.1
  36.6 1.3 copy-done.1
  38.0 0.0 collective-permute-done
  38.0 0.6 copy.13
  38.5 16.3 %shard_map.100 = bf16[2,4,32,4096]{3,2,1,0:T(8,128)(2,1)S(1)} custom-call(s32[2,32]{1,0:T(2,128)S(1)} %pad_add_fusion.delays_ref, bf16[2,32,256,128]{3,2,1,0:T(8,128)(2,1)S(1)} %bitcast.36, bf16[2,32,128,128]{3,2,1,0:T(8,128)(2,1)S(1)} %bitcast.39, f32[4,32,128]{2,1,0:T(8,128)S(1)} %bitcast.43, bf16[128,128]{1,0:T(8,128)(2,1)S(1)} %copy-done.4, ...), custom_call_target="tpu_custom_call" | custom-call | flops 8000000000 | bytes 8388608 | tf_op jit(solution)/shard_map/pallas_call | solution.py:273
  54.9 21.9 %shard_map.102 = bf16[8,512,512]{2,1,0:T(8,128)(2,1)} custom-call(s32[8,1,512]{2,1,0:T(1,128)S(1)} %reshape.96.picked_ref, bf16[256,4096]{1,0:T(8,128)(2,1)S(1)} %bitcast.41, bf16[256,4096]{1,0:T(8,128)(2,1)} %bitcast.40), custom_call_target="tpu_custom_call" | custom-call | tf_op jit(solution)/shard_map/pallas_call | solution.py:314
  76.8 52.6 %all_to_all.5 = bf16[8,512,512]{2,1,0:T(8,128)(2,1)S(1)} all-to-all(bf16[8,512,512]{2,1,0:T(8,128)(2,1)} %shard_map.102), channel_id=1, replica_groups={{0,1,2,3,4,5,6,7},{8,9,10,11,12,13,14,15},{16,17,18,19,20,21,22,23},{24..., dimensions={0} | all-to-all | bytes 8388608 | tf_op jit(solution)/shard_map/all_to_all | solution.py:328
  129.4 13.9 %shard_map.104 = bf16[1,1056,256]{2,1,0:T(8,128)(2,1)S(1)} custom-call(bf16[8,2,2,4,32,512]{5,4,3,2,1,0:T(8,128)(2,1)S(1)} %bitcast.37), custom_call_target="tpu_custom_call" | custom-call | flops 8000000000 | bytes 8388608 | tf_op jit(solution)/shard_map/pallas_call | solution.py:339
  143.4 2.3 %collective-permute-start.2 = (bf16[1,1056,256]{2,1,0:T(8,128)(2,1)S(1)}, bf16[1,1056,256]{2,1,0:T(8,128)(2,1)S(1)}, u32[]{:S(2)}, u32[]{:S(2)}) collective-permute-start(bf16[1,1056,256]{2,1,0:T(8,128)(2,1)S(1)} %shard_map.104), channel_id=1, source_target_pairs={{0,8},{1,9},{2,10},{3,11},{4,12},{5,13},{6,14},{7,15},{8,0},{9,1},... | collective-permute-start | bytes 1622024 | tf_op jit(solution)/shard_map/ppermute | solution.py:370
  145.7 13.9 %shard_map.103 = bf16[1,1056,256]{2,1,0:T(8,128)(2,1)S(1)} custom-call(bf16[8,2,2,4,32,512]{5,4,3,2,1,0:T(8,128)(2,1)S(1)} %bitcast.38), custom_call_target="tpu_custom_call" | custom-call | flops 8000000000 | bytes 8388608 | tf_op jit(solution)/shard_map/pallas_call | solution.py:339
  159.7 10.2 %collective-permute-done.2 = bf16[1,1056,256]{2,1,0:T(8,128)(2,1)S(1)} collective-permute-done((bf16[1,1056,256]{2,1,0:T(8,128)(2,1)S(1)}, bf16[1,1056,256]{2,1,0:T(8,128)(2,1)S(1)}, u32[]{:S(2)}, u32[]{:S(2)}) %collective-permute-start.2) | collective-permute-done | bytes 540704 | tf_op jit(solution)/shard_map/ppermute | solution.py:370
  169.9 0.1 pad_maximum_fusion.packed_ref
  170.0 3.6 %shard_map.105 = f32[2,2,256,1024]{3,2,1,0:T(8,128)} custom-call(s32[1]{0:T(128)} %bitcast.own_ref, bf16[2,1056,256]{2,1,0:T(8,128)(2,1)S(1)} %pad_maximum_fusion.packed_ref), custom_call_target="tpu_custom_call" | custom-call | tf_op jit(solution)/shard_map/pallas_call | solution.py:374
  (15 shorter events, 0.2 us)
Async XLA Ops:
  0.0 10.2 %copy-start.9 = (bf16[2,32,1]{1,0,2:T(2,128)(2,1)S(1)}, bf16[2,32,1]{1,0,2:T(2,128)(2,1)}, u32[]{:S(2)}) copy-start(bf16[2,32,1]{1,0,2:T(2,128)(2,1)} %param.11) | copy-start | bytes 388
  0.0 16.8 %collective-permute-start.1 = (bf16[2,32,1]{1,0,2:T(2,128)(2,1)}, bf16[2,32,1]{1,0,2:T(2,128)(2,1)S(1)}, u32[]{:S(2)}, u32[]{:S(2)}) collective-permute-start(bf16[2,32,1]{1,0,2:T(2,128)(2,1)} %param.11), channel_id=1, source_target_pairs={{0,1},{1,2},{2,3},{3,4},{4,5},{5,6},{6,7},{7,8},{8,9},{9,10},{10,1... | collective-permute-start | bytes 392 | tf_op jit(solution)/shard_map/ppermute | solution.py:234
  5.6 32.4 %collective-permute-start = (bf16[2,32,16384]{2,1,0:T(8,128)(2,1)}, bf16[2,32,16384]{2,1,0:T(8,128)(2,1)S(1)}, u32[]{:S(2)}, u32[]{:S(2)}) collective-permute-start(bf16[2,32,16384]{2,1,0:T(8,128)(2,1)} %slice.9), channel_id=1, source_target_pairs={{0,1},{1,2},{2,3},{3,4},{4,5},{5,6},{6,7},{7,8},{8,9},{9,10},{10,1... | collective-permute-start | bytes 6291464 | tf_op jit(solution)/shard_map/ppermute | solution.py:234
  10.3 5.6 %copy-start.7 = (f32[4,4096]{1,0:T(4,128)S(1)}, f32[4,4096]{1,0:T(4,128)}, u32[]{:S(2)}) copy-start(f32[4,4096]{1,0:T(4,128)} %param.14) | copy-start | bytes 196612
  10.3 5.6 %copy-start.8 = (s32[4096]{0:T(1024)S(1)}, s32[4096]{0:T(1024)}, u32[]{:S(2)}) copy-start(s32[4096]{0:T(1024)} %param.13) | copy-start | bytes 49156
  10.3 7.8 %copy-start.2 = (bf16[256,256]{1,0:T(8,128)(2,1)S(1)}, bf16[256,256]{1,0:T(8,128)(2,1)}, u32[]{:S(2)}) copy-start(bf16[256,256]{1,0:T(8,128)(2,1)} %constant.109.clone.w2h_ref) | copy-start | bytes 393220
  10.4 7.8 %copy-start.3 = (bf16[256,256]{1,0:T(8,128)(2,1)S(1)}, bf16[256,256]{1,0:T(8,128)(2,1)}, u32[]{:S(2)}) copy-start(bf16[256,256]{1,0:T(8,128)(2,1)} %constant.110.clone.w2l_ref) | copy-start | bytes 393220
  10.4 7.8 %copy-start.4 = (bf16[128,128]{1,0:T(8,128)(2,1)S(1)}, bf16[128,128]{1,0:T(8,128)(2,1)}, u32[]{:S(2)}) copy-start(bf16[128,128]{1,0:T(8,128)(2,1)} %constant.106.clone.w1h_ref) | copy-start | bytes 98308
  10.4 7.8 %copy-start.5 = (bf16[128,128]{1,0:T(8,128)(2,1)S(1)}, bf16[128,128]{1,0:T(8,128)(2,1)}, u32[]{:S(2)}) copy-start(bf16[128,128]{1,0:T(8,128)(2,1)} %constant.107.clone.w1l_ref) | copy-start | bytes 98308
  10.4 7.7 %copy-start.6 = (f32[2,32,128]{2,1,0:T(8,128)S(1)}, f32[2,32,128]{2,1,0:T(8,128)}, u32[]{:S(2)}) copy-start(f32[2,32,128]{2,1,0:T(8,128)} %constant.108.clone.twist_ref) | copy-start | bytes 98308
  18.2 2.2 %copy-start = (bf16[8,8,256,128]{3,2,1,0:T(8,128)(2,1)S(1)}, bf16[8,8,256,128]{3,2,1,0:T(8,128)(2,1)}, u32[]{:S(2)}) copy-start(bf16[8,8,256,128]{3,2,1,0:T(8,128)(2,1)} %copy.12) | copy-start | bytes 12582916
  36.6 1.3 copy-start.1
  143.4 26.5 %collective-permute-start.2 = (bf16[1,1056,256]{2,1,0:T(8,128)(2,1)S(1)}, bf16[1,1056,256]{2,1,0:T(8,128)(2,1)S(1)}, u32[]{:S(2)}, u32[]{:S(2)}) collective-permute-start(bf16[1,1056,256]{2,1,0:T(8,128)(2,1)S(1)} %shard_map.104), channel_id=1, source_target_pairs={{0,8},{1,9},{2,10},{3,11},{4,12},{5,13},{6,14},{7,15},{8,0},{9,1},... | collective-permute-start | bytes 1622024 | tf_op jit(solution)/shard_map/ppermute | solution.py:370

commit v5 on v4

--- a/solution.py
+++ b/solution.py
@@ -15,6 +15,7 @@
 GROUP = 8
 SUB = 8
 ROWS = 4
+TOGETHER = 4
 
 
 def block_matrix(size, scale):
@@ -98,12 +99,12 @@
                 turned_re[place, :] = real * twist_ref[0] - imag * twist_ref[1]
                 turned_im[place, :] = real * twist_ref[1] + imag * twist_ref[0]
 
-    def two_stations(pair, carry):
-        station(2 * pair, 0)
-        station(2 * pair + 1, 2)
+    def some_stations(pair, carry):
+        for step in range(TOGETHER):
+            station(TOGETHER * pair + step, 2 * step)
         return carry
 
-    lax.fori_loop(0, GROUP // 2, two_stations, 0)
+    lax.fori_loop(0, GROUP // TOGETHER, some_stations, 0)
     batch = 16
     e2_cos = e2_ref[0].reshape(rows, LANES)
     e2_sin = e2_ref[1].reshape(rows, LANES)
@@ -289,8 +290,8 @@
             out_specs=pl.BlockSpec((2, part_frames, GROUP, channels), lambda g: (0, 0, g, 0)),
             out_shape=jax.ShapeDtypeStruct((2, part_frames, stations, channels), jnp.bfloat16),
             scratch_shapes=[
-                pltpu.VMEM((4, (part_frames + TAPS) * radix + 8, LANES), jnp.float32),
-                pltpu.VMEM((4, (part_frames + TAPS - 1) * radix, LANES), jnp.float32),
+                pltpu.VMEM((2 * TOGETHER, (part_frames + TAPS) * radix + 8, LANES), jnp.float32),
+                pltpu.VMEM((2 * TOGETHER, (part_frames + TAPS - 1) * radix, LANES), jnp.float32),
                 pltpu.VMEM((radix * rows, LANES), jnp.float32),
                 pltpu.VMEM((radix * rows, LANES), jnp.float32),
             ],

time: 174 us -> 169 us (0.971)
  Pallas kernels: 86 us -> 81 us
    pallas_call x2, Pallas kernels: 32.6 us -> 27.6 us  [spectra(): pl.pallas_call(partial(spectra_kernel, which), grid=(stations // GROUP,),...]
  transfers between devices with their start and end apart: 3 -> 3, of which waited for: 1 -> 1; matrix products, arithmetic and copies ran while one was open for 6% -> 6% of each run, Pallas kernels for 17% -> 16%
where the time goes in v5:
time: 169 us; the launch traced here: 168 us
  Pallas kernels  81 us (48%)
  blocking collectives  52.5 us (31%)
  local copies, waits for them, and re-layouts  13.5 us (8%)
  waiting for transfers between devices  10.2 us (6%)
  starting transfers between devices  9.54 us (6%)
    all_to_all x1, blocking collectives, shards(): lax.all_to_all(packed, 'row', split_axis=0, concat_axis=0, tiled=True, ax...  52.5 us
    pallas_call x2, Pallas kernels, correlate(): pl.pallas_call(correlate_kernel, grid=(per,), in_specs=[pl.BlockSpec((mem...  27.9 us
    pallas_call x2, Pallas kernels, spectra(): pl.pallas_call(partial(spectra_kernel, which), grid=(stations // GROUP,),...  27.6 us
    pallas_call x1, Pallas kernels, shards(): pl.pallas_call(reorder_kernel, grid=(members,), in_specs=[pl.BlockSpec((1...  21.9 us
    ppermute x1, waiting for transfers between devices, shards(): product = lax.ppermute(product, 'row', route)  10.1 us
    unnamed x23, local copies, waits for them, and re-layouts  9.6 us
    ppermute x2, starting transfers between devices, shards(): lax.ppermute((samples[:, :, seg_len - tail_len:], delay_knots), 'row', ro...  7.13 us
    pallas_call x1, Pallas kernels, shards(): pl.pallas_call(spread_kernel, grid_spec=pltpu.PrefetchScalarGridSpec(num_...  3.59 us
  transfers between devices with their start and end apart: 3, of which 1 were waited for; matrix products, arithmetic and copies ran while one was open for 6% of the time, Pallas kernels for 16%

profile of v5, /device:TPU:0, one launch (start us, length us, event | category | flops | bytes accessed | tf_op | source)
XLA Modules:
  0.0 168.5 jit_solution(5099019812215119380)
XLA Ops:
  0.0 0.0 copy-start.9
  0.0 2.5 %collective-permute-start.1 = (bf16[2,32,1]{1,0,2:T(2,128)(2,1)}, bf16[2,32,1]{1,0,2:T(2,128)(2,1)S(1)}, u32[]{:S(2)}, u32[]{:S(2)}) collective-permute-start(bf16[2,32,1]{1,0,2:T(2,128)(2,1)} %param.11), channel_id=1, source_target_pairs={{0,1},{1,2},{2,3},{3,4},{4,5},{5,6},{6,7},{7,8},{8,9},{9,10},{10,1... | collective-permute-start | bytes 392 | tf_op jit(solution)/shard_map/ppermute | solution.py:235
  2.5 3.1 %slice.9 = bf16[2,32,16384]{2,1,0:T(8,128)(2,1)} slice(bf16[2,32,32768]{2,1,0:T(8,128)(2,1)} %param.10), slice={[0:2], [0:32], [16384:32768]} | slice | bytes 4194304 | tf_op jit(solution)/shard_map/slice | solution.py:235
  5.6 4.7 %collective-permute-start = (bf16[2,32,16384]{2,1,0:T(8,128)(2,1)}, bf16[2,32,16384]{2,1,0:T(8,128)(2,1)S(1)}, u32[]{:S(2)}, u32[]{:S(2)}) collective-permute-start(bf16[2,32,16384]{2,1,0:T(8,128)(2,1)} %slice.9), channel_id=1, source_target_pairs={{0,1},{1,2},{2,3},{3,4},{4,5},{5,6},{6,7},{7,8},{8,9},{9,10},{10,1... | collective-permute-start | bytes 6291464 | tf_op jit(solution)/shard_map/ppermute | solution.py:235
  10.2 0.0 copy-done.9
  10.3 0.0 copy-start.7
  10.3 0.0 copy-start.8
  10.3 0.0 copy-start.2
  10.4 0.0 copy-start.3
  10.4 0.0 copy-start.4
  10.4 0.0 copy-start.5
  10.4 0.0 copy-start.6
  10.4 5.5 %copy.12 = bf16[8,8,256,128]{3,2,1,0:T(8,128)(2,1)} copy(bf16[8,8,256,128]{3,1,2,0:T(8,128)(2,1)} %bitcast.44) | data formatting | bytes 8388608
  15.9 0.0 copy-done.7
  15.9 0.0 copy-done.8
  16.0 0.8 fusion.11
  16.8 0.0 collective-permute-done.1
  16.9 0.1 multiply_add_fusion.1
  16.9 0.6 fusion.1
  17.5 0.5 multiply_cosine_fusion
  18.1 0.0 copy-done.2
  18.1 0.0 copy-done.3
  18.1 0.0 copy-done.4
  18.1 0.0 copy-done.5
  18.1 0.0 copy-done.6
  18.2 0.0 copy-start
  18.2 2.2 %copy-done = bf16[8,8,256,128]{3,2,1,0:T(8,128)(2,1)S(1)} copy-done((bf16[8,8,256,128]{3,2,1,0:T(8,128)(2,1)S(1)}, bf16[8,8,256,128]{3,2,1,0:T(8,128)(2,1)}, u32[]{:S(2)}) %copy-start) | copy-done | bytes 4194328
  20.3 13.9 %shard_map.101 = bf16[2,4,32,4096]{3,2,1,0:T(8,128)(2,1)S(1)} custom-call(s32[2,32]{1,0:T(2,128)S(1)} %pad_add_fusion.delays_ref, bf16[2,32,256,128]{3,2,1,0:T(8,128)(2,1)S(1)} %bitcast.34, bf16[2,32,256,128]{3,2,1,0:T(8,128)(2,1)S(1)} %bitcast.35, f32[4,32,128]{2,1,0:T(8,128)S(1)} %bitcast.42, bf16[128,128]{1,0:T(8,128)(2,1)S(1)} %copy-done.4, ...), custom_call_target="tpu_custom_call" | custom-call | flops 8000000000 | bytes 8388608 | tf_op jit(solution)/shard_map/pallas_call | solution.py:274
  34.2 0.0 copy-start.1
  34.2 1.3 copy-done.1
  35.5 0.0 collective-permute-done
  35.5 0.6 copy.13
  36.1 13.8 %shard_map.100 = bf16[2,4,32,4096]{3,2,1,0:T(8,128)(2,1)S(1)} custom-call(s32[2,32]{1,0:T(2,128)S(1)} %pad_add_fusion.delays_ref, bf16[2,32,256,128]{3,2,1,0:T(8,128)(2,1)S(1)} %bitcast.36, bf16[2,32,128,128]{3,2,1,0:T(8,128)(2,1)S(1)} %bitcast.39, f32[4,32,128]{2,1,0:T(8,128)S(1)} %bitcast.43, bf16[128,128]{1,0:T(8,128)(2,1)S(1)} %copy-done.4, ...), custom_call_target="tpu_custom_call" | custom-call | flops 8000000000 | bytes 8388608 | tf_op jit(solution)/shard_map/pallas_call | solution.py:274
  49.9 21.9 %shard_map.102 = bf16[8,512,512]{2,1,0:T(8,128)(2,1)} custom-call(s32[8,1,512]{2,1,0:T(1,128)S(1)} %reshape.96.picked_ref, bf16[256,4096]{1,0:T(8,128)(2,1)S(1)} %bitcast.41, bf16[256,4096]{1,0:T(8,128)(2,1)} %bitcast.40), custom_call_target="tpu_custom_call" | custom-call | tf_op jit(solution)/shard_map/pallas_call | solution.py:315
  71.8 52.5 %all_to_all.5 = bf16[8,512,512]{2,1,0:T(8,128)(2,1)S(1)} all-to-all(bf16[8,512,512]{2,1,0:T(8,128)(2,1)} %shard_map.102), channel_id=1, replica_groups={{0,1,2,3,4,5,6,7},{8,9,10,11,12,13,14,15},{16,17,18,19,20,21,22,23},{24..., dimensions={0} | all-to-all | bytes 8388608 | tf_op jit(solution)/shard_map/all_to_all | solution.py:329
  124.4 13.9 %shard_map.104 = bf16[1,1056,256]{2,1,0:T(8,128)(2,1)S(1)} custom-call(bf16[8,2,2,4,32,512]{5,4,3,2,1,0:T(8,128)(2,1)S(1)} %bitcast.37), custom_call_target="tpu_custom_call" | custom-call | flops 8000000000 | bytes 8388608 | tf_op jit(solution)/shard_map/pallas_call | solution.py:340
  138.3 2.4 %collective-permute-start.2 = (bf16[1,1056,256]{2,1,0:T(8,128)(2,1)S(1)}, bf16[1,1056,256]{2,1,0:T(8,128)(2,1)S(1)}, u32[]{:S(2)}, u32[]{:S(2)}) collective-permute-start(bf16[1,1056,256]{2,1,0:T(8,128)(2,1)S(1)} %shard_map.104), channel_id=1, source_target_pairs={{0,8},{1,9},{2,10},{3,11},{4,12},{5,13},{6,14},{7,15},{8,0},{9,1},... | collective-permute-start | bytes 1622024 | tf_op jit(solution)/shard_map/ppermute | solution.py:371
  140.7 13.9 %shard_map.103 = bf16[1,1056,256]{2,1,0:T(8,128)(2,1)S(1)} custom-call(bf16[8,2,2,4,32,512]{5,4,3,2,1,0:T(8,128)(2,1)S(1)} %bitcast.38), custom_call_target="tpu_custom_call" | custom-call | flops 8000000000 | bytes 8388608 | tf_op jit(solution)/shard_map/pallas_call | solution.py:340
  154.6 10.1 %collective-permute-done.2 = bf16[1,1056,256]{2,1,0:T(8,128)(2,1)S(1)} collective-permute-done((bf16[1,1056,256]{2,1,0:T(8,128)(2,1)S(1)}, bf16[1,1056,256]{2,1,0:T(8,128)(2,1)S(1)}, u32[]{:S(2)}, u32[]{:S(2)}) %collective-permute-start.2) | collective-permute-done | bytes 540704 | tf_op jit(solution)/shard_map/ppermute | solution.py:371
  164.8 0.1 pad_maximum_fusion.packed_ref
  164.9 3.6 %shard_map.105 = f32[2,2,256,1024]{3,2,1,0:T(8,128)} custom-call(s32[1]{0:T(128)} %bitcast.own_ref, bf16[2,1056,256]{2,1,0:T(8,128)(2,1)S(1)} %pad_maximum_fusion.packed_ref), custom_call_target="tpu_custom_call" | custom-call | tf_op jit(solution)/shard_map/pallas_call | solution.py:375
  (15 shorter events, 0.2 us)
Async XLA Ops:
  0.0 10.2 %copy-start.9 = (bf16[2,32,1]{1,0,2:T(2,128)(2,1)S(1)}, bf16[2,32,1]{1,0,2:T(2,128)(2,1)}, u32[]{:S(2)}) copy-start(bf16[2,32,1]{1,0,2:T(2,128)(2,1)} %param.11) | copy-start | bytes 388
  0.0 16.8 %collective-permute-start.1 = (bf16[2,32,1]{1,0,2:T(2,128)(2,1)}, bf16[2,32,1]{1,0,2:T(2,128)(2,1)S(1)}, u32[]{:S(2)}, u32[]{:S(2)}) collective-permute-start(bf16[2,32,1]{1,0,2:T(2,128)(2,1)} %param.11), channel_id=1, source_target_pairs={{0,1},{1,2},{2,3},{3,4},{4,5},{5,6},{6,7},{7,8},{8,9},{9,10},{10,1... | collective-permute-start | bytes 392 | tf_op jit(solution)/shard_map/ppermute | solution.py:235
  5.6 30.0 %collective-permute-start = (bf16[2,32,16384]{2,1,0:T(8,128)(2,1)}, bf16[2,32,16384]{2,1,0:T(8,128)(2,1)S(1)}, u32[]{:S(2)}, u32[]{:S(2)}) collective-permute-start(bf16[2,32,16384]{2,1,0:T(8,128)(2,1)} %slice.9), channel_id=1, source_target_pairs={{0,1},{1,2},{2,3},{3,4},{4,5},{5,6},{6,7},{7,8},{8,9},{9,10},{10,1... | collective-permute-start | bytes 6291464 | tf_op jit(solution)/shard_map/ppermute | solution.py:235
  10.3 5.6 %copy-start.7 = (f32[4,4096]{1,0:T(4,128)S(1)}, f32[4,4096]{1,0:T(4,128)}, u32[]{:S(2)}) copy-start(f32[4,4096]{1,0:T(4,128)} %param.14) | copy-start | bytes 196612
  10.3 5.6 %copy-start.8 = (s32[4096]{0:T(1024)S(1)}, s32[4096]{0:T(1024)}, u32[]{:S(2)}) copy-start(s32[4096]{0:T(1024)} %param.13) | copy-start | bytes 49156
  10.3 7.8 %copy-start.2 = (bf16[256,256]{1,0:T(8,128)(2,1)S(1)}, bf16[256,256]{1,0:T(8,128)(2,1)}, u32[]{:S(2)}) copy-start(bf16[256,256]{1,0:T(8,128)(2,1)} %constant.109.clone.w2h_ref) | copy-start | bytes 393220
  10.4 7.8 %copy-start.3 = (bf16[256,256]{1,0:T(8,128)(2,1)S(1)}, bf16[256,256]{1,0:T(8,128)(2,1)}, u32[]{:S(2)}) copy-start(bf16[256,256]{1,0:T(8,128)(2,1)} %constant.110.clone.w2l_ref) | copy-start | bytes 393220
  10.4 7.8 %copy-start.4 = (bf16[128,128]{1,0:T(8,128)(2,1)S(1)}, bf16[128,128]{1,0:T(8,128)(2,1)}, u32[]{:S(2)}) copy-start(bf16[128,128]{1,0:T(8,128)(2,1)} %constant.106.clone.w1h_ref) | copy-start | bytes 98308
  10.4 7.8 %copy-start.5 = (bf16[128,128]{1,0:T(8,128)(2,1)S(1)}, bf16[128,128]{1,0:T(8,128)(2,1)}, u32[]{:S(2)}) copy-start(bf16[128,128]{1,0:T(8,128)(2,1)} %constant.107.clone.w1l_ref) | copy-start | bytes 98308
  10.4 7.7 %copy-start.6 = (f32[2,32,128]{2,1,0:T(8,128)S(1)}, f32[2,32,128]{2,1,0:T(8,128)}, u32[]{:S(2)}) copy-start(f32[2,32,128]{2,1,0:T(8,128)} %constant.108.clone.twist_ref) | copy-start | bytes 98308
  18.2 2.2 %copy-start = (bf16[8,8,256,128]{3,2,1,0:T(8,128)(2,1)S(1)}, bf16[8,8,256,128]{3,2,1,0:T(8,128)(2,1)}, u32[]{:S(2)}) copy-start(bf16[8,8,256,128]{3,2,1,0:T(8,128)(2,1)} %copy.12) | copy-start | bytes 12582916
  34.2 1.3 copy-start.1
  138.3 26.5 %collective-permute-start.2 = (bf16[1,1056,256]{2,1,0:T(8,128)(2,1)S(1)}, bf16[1,1056,256]{2,1,0:T(8,128)(2,1)S(1)}, u32[]{:S(2)}, u32[]{:S(2)}) collective-permute-start(bf16[1,1056,256]{2,1,0:T(8,128)(2,1)S(1)} %shard_map.104), channel_id=1, source_target_pairs={{0,8},{1,9},{2,10},{3,11},{4,12},{5,13},{6,14},{7,15},{8,0},{9,1},... | collective-permute-start | bytes 1622024 | tf_op jit(solution)/shard_map/ppermute | solution.py:371
